TPU v7x, 32 devices: a whole 2x2x4 slice. The times are simulated.
32 devices in a mesh: grp: 4 (over z), fsdp: 4 (over x, core), tp: 2 (over y).
Axes of the slice: x: 2, y: 2, z: 4, core: 2. Of those that a mesh axis runs over, the one named last changes fastest.
Arguments:
- hidden_in: bfloat16 [6144, 1024], P(('grp', 'fsdp', 'tp')), may hold values from -6 to 6
- lengths: int32 [16], P(('grp', 'fsdp')), may hold values from 96 to 384, as said below
- norm1_gain: float32 [1024], replicated, may hold values from 0.1 to 1.9
- w_query: bfloat16 [1024, 512], P('fsdp', 'tp'), may hold values from -0.1875 to 0.1875
- key_weight: bfloat16 [1024, 128], P('fsdp', 'tp'), may hold values from -0.1875 to 0.1875
- value_weight: bfloat16 [1024, 128], P('fsdp', 'tp'), may hold values from -0.1875 to 0.1875
- w_attn_out: bfloat16 [1024, 512], P('fsdp', 'tp'), may hold values from -0.75 to 0.75
- w_mamba_z: bfloat16 [1024, 1536], P('fsdp', 'tp'), may hold values from -0.1875 to 0.1875
- w_mamba_x: bfloat16 [1024, 1536], P('fsdp', 'tp'), may hold values from -0.1875 to 0.1875
- w_step: bfloat16 [1024, 24], P('fsdp', 'tp'), may hold values from -0.1875 to 0.1875
- w_shared: bfloat16 [1024, 256], replicated, may hold values from -0.1875 to 0.1875
- conv_main: float32 [4, 1536], replicated, may hold values from -3 to 3
- conv_shared: float32 [4, 256], replicated, may hold values from -3 to 3
- decay_log: float32 [24], replicated, may hold values from -4 to 0.5
- step_bias: float32 [24], replicated, may hold values from -4.5 to -2
- skip_gain: float32 [24], replicated, may hold values from 0.5 to 1.5
- w_mamba_out: bfloat16 [1024, 1536], P('fsdp', 'tp'), may hold values from -0.25 to 0.25
- norm2_gain: float32 [1024], replicated, may hold values from 0.1 to 1.9
- w_ffn_gate: bfloat16 [1024, 2048], P('fsdp', 'tp'), may hold values from -0.1875 to 0.1875
- w_ffn_up: bfloat16 [1024, 2048], P('fsdp', 'tp'), may hold values from -0.1875 to 0.1875
- w_ffn_down: bfloat16 [1024, 2048], P('fsdp', 'tp'), may hold values from -0.1875 to 0.1875
- out_grad: bfloat16 [6144, 1024], P(('grp', 'fsdp', 'tp')), may hold values from -6 to 6
Outputs:
- output: bfloat16 [6144, 1024], P(('grp', 'fsdp', 'tp'))
- grad_in: bfloat16 [6144, 1024], P(('grp', 'fsdp', 'tp'))
- grad_norm1: float32 [1024], replicated
- grad_query: float32 [1024, 512], P(('grp', 'fsdp'), 'tp')
- grad_key: float32 [1024, 128], P(('grp', 'fsdp'), 'tp')
- grad_value: float32 [1024, 128], P(('grp', 'fsdp'), 'tp')
- grad_attn_out: float32 [1024, 512], P(('grp', 'fsdp'), 'tp')
- grad_mamba_z: float32 [1024, 1536], P(('grp', 'fsdp'), 'tp')
- grad_mamba_x: float32 [1024, 1536], P(('grp', 'fsdp'), 'tp')
- grad_step: float32 [1024, 24], P(('grp', 'fsdp'), 'tp')
- grad_shared: float32 [1024, 256], replicated
- grad_conv_main: float32 [4, 1536], replicated
- grad_conv_shared: float32 [4, 256], replicated
- grad_decay_log: float32 [24], replicated
- grad_step_bias: float32 [24], replicated
- grad_skip_gain: float32 [24], replicated
- grad_mamba_out: float32 [1024, 1536], P(('grp', 'fsdp'), 'tp')
- grad_norm2: float32 [1024], replicated
- grad_ffn_gate: float32 [1024, 2048], P(('grp', 'fsdp'), 'tp')
- grad_ffn_up: float32 [1024, 2048], P(('grp', 'fsdp'), 'tp')
- grad_ffn_down: float32 [1024, 2048], P(('grp', 'fsdp'), 'tp')
Inputs may be any that keep to these rules, and one draw needn't show every extreme that they name: `lengths`: each sequence's valid slots come first; some sequence has all 384 slots valid.
All inputs are finite; a program needn't handle non-finite values.
Results may differ from a plain program's by a relative error of at most 0.011.
Values may be sent and summed in bfloat16 or wider, within the bound.
A program may use at most 128 MiB of HBM per device.

v0:
```python
from functools import partial

import jax
import jax.numpy as jnp
from jax import lax
from jax.sharding import PartitionSpec as P

HEAD_DIMENSION = 64
BLOCK = 128


top_precision = lax.Precision.HIGHEST
norm_eps = 1e-05
rope_base = 100000000000.0


def for_sending(shard):

    def short(part):
        return part.astype(jnp.bfloat16) if part.dtype == jnp.float32 else part

    return jax.tree.map(short, shard)


def dot_nt(first_mat, second_mat):
    return lax.dot_general(
        first_mat, second_mat, (((1,), (1,)), ((), ())), preferred_element_type=jnp.float32
    )


def dot_tn(first_mat, second_mat):
    return lax.dot_general(
        first_mat, second_mat, (((0,), (0,)), ((), ())), preferred_element_type=jnp.float32
    )


def rms_scale(values):
    return lax.rsqrt(jnp.mean(values * values, axis=-1, keepdims=True) + norm_eps)


def angles(length_total, head_size):
    positions = jnp.arange(length_total).astype(jnp.float32)[:, None]
    exponent = jnp.arange(head_size // 2).astype(jnp.float32) * (-2.0 / head_size)
    phase = positions * jnp.power(rope_base, exponent)[None, :]
    return (jnp.cos(phase)[:, None, :], jnp.sin(phase)[:, None, :])


def apply_rotary(values, rotary_cosine, rotary_sine):
    half_dim = values.shape[-1] // 2
    first_half = values[..., :half_dim]
    second_half = values[..., half_dim:]
    return jnp.concatenate(
        [
            first_half * rotary_cosine - second_half * rotary_sine,
            second_half * rotary_cosine + first_half * rotary_sine,
        ],
        axis=-1,
    )


def rotate_back(grads, rotary_cosine, rotary_sine):
    half_dim = grads.shape[-1] // 2
    first_half = grads[..., :half_dim]
    second_half = grads[..., half_dim:]
    return jnp.concatenate(
        [
            first_half * rotary_cosine + second_half * rotary_sine,
            second_half * rotary_cosine - first_half * rotary_sine,
        ],
        axis=-1,
    )


def causal_conv(values, kernel):
    kernel_width = kernel.shape[0]
    length_total = values.shape[0]
    padded = jnp.pad(values, ((kernel_width - 1, 0), (0, 0)))
    result = kernel[kernel_width - 1] * values
    for offset in range(kernel_width - 1):
        result = result + kernel[offset] * padded[offset : offset + length_total]
    return result


def state_scan(x_heads, step_sizes, rates, b_matrix, c_matrix):
    length_total, head_count, head_size = x_heads.shape
    nstate = b_matrix.shape[1]
    blocks = length_total // BLOCK
    xs_blk = x_heads.reshape(blocks, BLOCK, head_count, head_size)
    step_blk = step_sizes.reshape(blocks, BLOCK, head_count)
    b_blk = b_matrix.reshape(blocks, BLOCK, nstate)
    c_blk = c_matrix.reshape(blocks, BLOCK, nstate)
    cumulative = jnp.cumsum(step_blk * rates, axis=1)
    index_t = jnp.arange(BLOCK)
    causal = (index_t[:, None] >= index_t[None, :])[None, :, :, None]
    log_gaps = cumulative[:, :, None, :] - cumulative[:, None, :, :]
    decay_mat = jnp.where(causal, jnp.exp(jnp.where(causal, log_gaps, 0.0)), 0.0)
    inner_prod = jnp.einsum("ctn,csn->cts", c_blk, b_blk, precision=top_precision)
    mixing = decay_mat * inner_prod[:, :, :, None] * step_blk[:, None, :, :]
    within = jnp.einsum("ctsh,cshp->cthp", mixing, xs_blk, precision=top_precision)
    tail_weight = jnp.exp(cumulative[:, -1:, :] - cumulative) * step_blk
    states = jnp.einsum("csh,csn,cshp->chpn", tail_weight, b_blk, xs_blk, precision=top_precision)
    fading = jnp.exp(cumulative[:, -1, :])

    def advance(state_carry, pieces):
        fade_now, state_now = pieces
        return (fade_now[:, None, None] * state_carry + state_now, state_carry)

    _, before = lax.scan(
        advance, jnp.zeros((head_count, head_size, nstate), jnp.float32), (fading, states)
    )
    across = (
        jnp.einsum("ctn,chpn->cthp", c_blk, before, precision=top_precision)
        * jnp.exp(cumulative)[:, :, :, None]
    )
    return (within + across).reshape(length_total, head_count, head_size)


def mamba_mix(
    gate_in,
    main_in,
    shared_in,
    step_in,
    kernel_main,
    kernel_shared,
    decay_rates,
    bias_step,
    skip_terms,
    valid_rows,
):
    length_total = main_in.shape[0]
    head_count = step_in.shape[1]
    head_size = main_in.shape[1] // head_count
    nstate = shared_in.shape[1] // 2
    main_conv = jax.nn.silu(causal_conv(main_in, kernel_main))
    shared_conv = jax.nn.silu(causal_conv(shared_in, kernel_shared))
    step_sizes = jax.nn.softplus(step_in + bias_step) * valid_rows
    x_heads = main_conv.reshape(length_total, head_count, head_size)
    scanned = state_scan(
        x_heads, step_sizes, -jnp.exp(decay_rates), shared_conv[:, :nstate], shared_conv[:, nstate:]
    )
    output_heads = scanned + skip_terms[:, None] * x_heads
    return output_heads.reshape(length_total, head_count * head_size) * jax.nn.silu(gate_in)


def gather_weights(weights):
    return jax.tree.map(
        lambda part, own: part.astype(own.dtype),
        lax.all_gather(for_sending(weights), "fsdp", axis=0, tiled=True),
        weights,
    )


def gather_again(weights):
    return jax.tree.map(
        lambda part, own: part.astype(own.dtype),
        lax.all_gather(for_sending(weights), "fsdp", axis=0, tiled=True),
        weights,
    )


def reduce_weight_grads(term_fn, model_width):
    group_count = lax.axis_size("grp")
    fsdp_count = lax.axis_size("fsdp")
    return lax.psum_scatter(
        term_fn(
            jnp.int32(0),
            lax.axis_size(("grp", "fsdp")) * (model_width // (group_count * fsdp_count)),
        ),
        ("grp", "fsdp"),
        scatter_dimension=0,
        tiled=True,
    )


def local(
    hidden_in,
    lengths,
    norm1_gain,
    w_query,
    key_weight,
    value_weight,
    w_attn_out,
    w_mamba_z,
    w_mamba_x,
    w_step,
    w_shared,
    conv_main,
    conv_shared,
    decay_log,
    step_bias,
    skip_gain,
    w_mamba_out,
    norm2_gain,
    w_ffn_gate,
    w_ffn_up,
    w_ffn_down,
    out_grad,
):
    tp_count = lax.axis_size("tp")
    tp_rank = lax.axis_index("tp")
    own_rows = hidden_in.shape[0]
    seq_len = own_rows * tp_count
    model_width = hidden_in.shape[1]
    valid_count = lengths[0]
    positions = jnp.arange(seq_len, dtype=jnp.int32)
    valid_full = (positions < valid_count).astype(jnp.float32)[:, None]
    valid_own = lax.dynamic_slice_in_dim(valid_full, tp_rank * own_rows, own_rows, 0)
    resid_in = hidden_in.astype(jnp.float32)
    scale_one = rms_scale(resid_in)
    first_normalized = (resid_in * scale_one * norm1_gain).astype(jnp.bfloat16)
    top_grad = out_grad.astype(jnp.float32) * valid_own
    top_grad_low = top_grad.astype(jnp.bfloat16)
    normed1_all, top_grad_all = (
        lax.all_gather(first_normalized, "tp", axis=0, tiled=True),
        lax.all_gather(top_grad_low, "tp", axis=0, tiled=True),
    )
    mixer_full = gather_weights(
        (w_query, key_weight, value_weight, w_attn_out, w_mamba_z, w_mamba_x, w_step, w_mamba_out)
    )
    ffn_full = gather_weights((w_ffn_gate, w_ffn_up, w_ffn_down))
    wq_all, wk_all, wv_all, wo_all, wz_all, wx_all, wdt_all, wout_all = mixer_full
    q_local = wq_all.shape[1] // HEAD_DIMENSION
    kv_local = wk_all.shape[1] // HEAD_DIMENSION
    grouping = q_local // kv_local
    attn_scale = HEAD_DIMENSION ** (-0.5)
    rotary_cosine, rotary_sine = angles(seq_len, HEAD_DIMENSION)
    query_projected = jnp.dot(normed1_all, wq_all, preferred_element_type=jnp.float32)
    key_projected = jnp.dot(normed1_all, wk_all, preferred_element_type=jnp.float32)
    value_proj = jnp.dot(normed1_all, wv_all, preferred_element_type=jnp.float32)
    query_rotated = apply_rotary(
        query_projected.reshape(seq_len, q_local, HEAD_DIMENSION), rotary_cosine, rotary_sine
    ).astype(jnp.bfloat16)
    key_rot = apply_rotary(
        key_projected.reshape(seq_len, kv_local, HEAD_DIMENSION), rotary_cosine, rotary_sine
    ).astype(jnp.bfloat16)
    value_reduced = value_proj.astype(jnp.bfloat16).reshape(seq_len, kv_local, HEAD_DIMENSION)
    query_grp = query_rotated.reshape(seq_len, kv_local, grouping, HEAD_DIMENSION)
    score_raw = (
        jnp.einsum("qkgd,skd->kgqs", query_grp, key_rot, preferred_element_type=jnp.float32)
        * attn_scale
    )
    allowed = (positions[:, None] >= positions[None, :]) & (positions[None, :] < valid_count)
    masked = jnp.where(allowed, score_raw, -1e30)
    peak_score = jnp.max(masked, axis=-1, keepdims=True)
    expo_score = jnp.exp(masked - peak_score)
    probs = expo_score / jnp.sum(expo_score, axis=-1, keepdims=True)
    probs_low = probs.astype(jnp.bfloat16)
    attn_heads = jnp.einsum(
        "kgqs,skd->qkgd", probs_low, value_reduced, preferred_element_type=jnp.float32
    )
    attn_low = attn_heads.reshape(seq_len, q_local * HEAD_DIMENSION).astype(jnp.bfloat16)
    heads_local = wdt_all.shape[1]
    inner_local = wx_all.shape[1]
    gate_proj = jnp.dot(normed1_all, wz_all, preferred_element_type=jnp.float32)
    main_proj = jnp.dot(normed1_all, wx_all, preferred_element_type=jnp.float32)
    step_proj = jnp.dot(normed1_all, wdt_all, preferred_element_type=jnp.float32)
    shared_proj = jnp.dot(normed1_all, w_shared, preferred_element_type=jnp.float32)
    kernel_local = lax.dynamic_slice_in_dim(conv_main, tp_rank * inner_local, inner_local, 1)
    decay_local = lax.dynamic_slice_in_dim(decay_log, tp_rank * heads_local, heads_local, 0)
    bias_local = lax.dynamic_slice_in_dim(step_bias, tp_rank * heads_local, heads_local, 0)
    skip_local = lax.dynamic_slice_in_dim(skip_gain, tp_rank * heads_local, heads_local, 0)
    mamba_out, mamba_pull = jax.vjp(
        partial(mamba_mix, valid_rows=valid_full),
        gate_proj,
        main_proj,
        shared_proj,
        step_proj,
        kernel_local,
        conv_shared,
        decay_local,
        bias_local,
        skip_local,
    )
    mamba_low = mamba_out.astype(jnp.bfloat16)
    mix_part = dot_nt(attn_low, wo_all) + dot_nt(mamba_low, wout_all)
    mixed = lax.psum_scatter(mix_part, "tp", scatter_dimension=0, tiled=True)
    resid_mid = resid_in + mixed
    scale_two = rms_scale(resid_mid)
    normed2 = (resid_mid * scale_two * norm2_gain).astype(jnp.bfloat16)
    normed2_all = lax.all_gather(normed2, "tp", axis=0, tiled=True)
    wg_all, wu_all, wd_all = ffn_full
    gate_pre = jnp.dot(normed2_all, wg_all, preferred_element_type=jnp.float32)
    up_pre = jnp.dot(normed2_all, wu_all, preferred_element_type=jnp.float32)
    sigma_gate = jax.nn.sigmoid(gate_pre)
    silu_gate = gate_pre * sigma_gate
    hidden_low = (silu_gate * up_pre).astype(jnp.bfloat16)
    ffn_part = dot_nt(hidden_low, wd_all)
    ffn_sum = lax.psum_scatter(
        ffn_part.astype(jnp.bfloat16), "tp", scatter_dimension=0, tiled=True
    ).astype(jnp.float32)
    output = ((resid_mid + ffn_sum) * valid_own).astype(jnp.bfloat16)
    ffn_back = gather_again((w_ffn_gate, w_ffn_up, w_ffn_down))
    wg_back, wu_back, wd_back = ffn_back
    hidden_grad = jnp.dot(top_grad_all, wd_back, preferred_element_type=jnp.float32)
    silu_slope = sigma_gate * (1.0 + gate_pre * (1.0 - sigma_gate))
    gate_grad = (hidden_grad * up_pre * silu_slope).astype(jnp.bfloat16)
    up_grad = (hidden_grad * silu_gate).astype(jnp.bfloat16)

    def ffn_terms(start, count):
        return jnp.concatenate(
            [
                dot_tn(normed2_all, gate_grad),
                dot_tn(normed2_all, up_grad),
                dot_tn(top_grad_all, hidden_low),
            ],
            axis=1,
        )

    ffn_grads = reduce_weight_grads(ffn_terms, model_width)
    norm2_part = dot_nt(gate_grad, wg_back) + dot_nt(up_grad, wu_back)
    norm2_grad = lax.psum_scatter(norm2_part, "tp", scatter_dimension=0, tiled=True)
    gain2_part = jnp.sum(norm2_grad * resid_mid * scale_two, axis=0)
    weighted2 = norm2_grad * norm2_gain
    resid_grad = (
        top_grad
        + scale_two * weighted2
        - resid_mid * scale_two**3 * jnp.mean(weighted2 * resid_mid, axis=-1, keepdims=True)
    )
    mix_grad_low = resid_grad.astype(jnp.bfloat16)
    mix_grad_all = lax.all_gather(mix_grad_low, "tp", axis=0, tiled=True)
    mixer_back = gather_again(
        (w_query, key_weight, value_weight, w_attn_out, w_mamba_z, w_mamba_x, w_step, w_mamba_out)
    )
    wq_back, wk_back, wv_back, wo_back, wz_back, wx_back, wdt_back, wout_back = mixer_back
    attn_grad = jnp.dot(mix_grad_all, wo_back, preferred_element_type=jnp.float32).astype(
        jnp.bfloat16
    )
    mamba_grad = jnp.dot(mix_grad_all, wout_back, preferred_element_type=jnp.float32)
    (
        gate_back,
        main_back,
        shared_back,
        step_back,
        kernel_grad,
        conv_shared_grad,
        decay_grad,
        bias_grad,
        skip_grad,
    ) = mamba_pull(mamba_grad)
    gate_back_low = gate_back.astype(jnp.bfloat16)
    main_back_low = main_back.astype(jnp.bfloat16)
    step_back_low = step_back.astype(jnp.bfloat16)
    attn_grad_heads = attn_grad.reshape(seq_len, kv_local, grouping, HEAD_DIMENSION)
    prob_grad = jnp.einsum(
        "qkgd,skd->kgqs", attn_grad_heads, value_reduced, preferred_element_type=jnp.float32
    )
    value_grad = jnp.einsum(
        "kgqs,qkgd->skd", probs_low, attn_grad_heads, preferred_element_type=jnp.float32
    )
    score_grad = (probs * (prob_grad - jnp.sum(probs * prob_grad, axis=-1, keepdims=True))).astype(
        jnp.bfloat16
    )
    query_grad = (
        jnp.einsum("kgqs,skd->qkgd", score_grad, key_rot, preferred_element_type=jnp.float32)
        * attn_scale
    )
    key_grad = (
        jnp.einsum("kgqs,qkgd->skd", score_grad, query_grp, preferred_element_type=jnp.float32)
        * attn_scale
    )
    query_back = (
        rotate_back(
            query_grad.reshape(seq_len, q_local, HEAD_DIMENSION), rotary_cosine, rotary_sine
        )
        .reshape(seq_len, q_local * HEAD_DIMENSION)
        .astype(jnp.bfloat16)
    )
    key_back = (
        rotate_back(key_grad, rotary_cosine, rotary_sine)
        .reshape(seq_len, kv_local * HEAD_DIMENSION)
        .astype(jnp.bfloat16)
    )
    value_back = value_grad.reshape(seq_len, kv_local * HEAD_DIMENSION).astype(jnp.bfloat16)
    shared_weight = w_shared.astype(jnp.float32)
    norm1_part = (
        dot_nt(query_back, wq_back)
        + dot_nt(key_back, wk_back)
        + dot_nt(value_back, wv_back)
        + dot_nt(gate_back_low, wz_back)
        + dot_nt(main_back_low, wx_back)
        + dot_nt(step_back_low, wdt_back)
        + lax.dot_general(
            shared_back,
            shared_weight,
            (((1,), (1,)), ((), ())),
            precision=top_precision,
            preferred_element_type=jnp.float32,
        )
    )
    norm1_grad = lax.psum_scatter(norm1_part, "tp", scatter_dimension=0, tiled=True)
    gain1_part = jnp.sum(norm1_grad * resid_in * scale_one, axis=0)
    weighted1 = norm1_grad * norm1_gain
    input_grad = (
        resid_grad
        + scale_one * weighted1
        - resid_in * scale_one**3 * jnp.mean(weighted1 * resid_in, axis=-1, keepdims=True)
    )
    grad_in = input_grad.astype(jnp.bfloat16)

    def mixer_terms(start, count):
        return jnp.concatenate(
            [
                dot_tn(normed1_all, query_back),
                dot_tn(normed1_all, key_back),
                dot_tn(normed1_all, value_back),
                dot_tn(mix_grad_all, attn_low),
                dot_tn(normed1_all, gate_back_low),
                dot_tn(normed1_all, main_back_low),
                dot_tn(normed1_all, step_back_low),
                dot_tn(mix_grad_all, mamba_low),
            ],
            axis=1,
        )

    mixer_grads = reduce_weight_grads(mixer_terms, model_width)
    shared_w_grad = lax.dot_general(
        normed1_all.astype(jnp.float32),
        shared_back,
        (((0,), (0,)), ((), ())),
        precision=top_precision,
        preferred_element_type=jnp.float32,
    )
    kernel_full = lax.dynamic_update_slice_in_dim(
        jnp.zeros(conv_main.shape, jnp.float32), kernel_grad, tp_rank * inner_local, 1
    )
    decay_full = lax.dynamic_update_slice_in_dim(
        jnp.zeros(decay_log.shape, jnp.float32), decay_grad, tp_rank * heads_local, 0
    )
    bias_full = lax.dynamic_update_slice_in_dim(
        jnp.zeros(step_bias.shape, jnp.float32), bias_grad, tp_rank * heads_local, 0
    )
    skip_full = lax.dynamic_update_slice_in_dim(
        jnp.zeros(skip_gain.shape, jnp.float32), skip_grad, tp_rank * heads_local, 0
    )
    gain1_sum, shared_sum, kernel_sum, conv_shared_sum, decay_sum, bias_sum, skip_sum, gain2_sum = (
        lax.psum(
            (
                gain1_part,
                shared_w_grad,
                kernel_full,
                conv_shared_grad,
                decay_full,
                bias_full,
                skip_full,
                gain2_part,
            ),
            ("grp", "fsdp", "tp"),
        )
    )
    mixer_widths = [
        wq_all.shape[1],
        wk_all.shape[1],
        wv_all.shape[1],
        wo_all.shape[1],
        wz_all.shape[1],
        wx_all.shape[1],
        wdt_all.shape[1],
        wout_all.shape[1],
    ]
    mixer_parts = []
    column = 0
    for width_now in mixer_widths:
        mixer_parts.append(mixer_grads[:, column : column + width_now])
        column = column + width_now
    ffn_width = wg_all.shape[1]
    return (
        output,
        grad_in,
        gain1_sum,
        mixer_parts[0],
        mixer_parts[1],
        mixer_parts[2],
        mixer_parts[3],
        mixer_parts[4],
        mixer_parts[5],
        mixer_parts[6],
        shared_sum,
        kernel_sum,
        conv_shared_sum,
        decay_sum,
        bias_sum,
        skip_sum,
        mixer_parts[7],
        gain2_sum,
        ffn_grads[:, :ffn_width],
        ffn_grads[:, ffn_width : 2 * ffn_width],
        ffn_grads[:, 2 * ffn_width :],
    )


def solution(mesh):
    placed = (
        P(("grp", "fsdp", "tp"), None),
        P(("grp", "fsdp")),
        P(),
        P("fsdp", "tp"),
        P("fsdp", "tp"),
        P("fsdp", "tp"),
        P("fsdp", "tp"),
        P("fsdp", "tp"),
        P("fsdp", "tp"),
        P("fsdp", "tp"),
        P(),
        P(),
        P(),
        P(),
        P(),
        P(),
        P("fsdp", "tp"),
        P(),
        P("fsdp", "tp"),
        P("fsdp", "tp"),
        P("fsdp", "tp"),
        P(("grp", "fsdp", "tp"), None),
    )
    return jax.shard_map(
        local,
        mesh=mesh,
        in_specs=placed,
        out_specs=(
            P(("grp", "fsdp", "tp"), None),
            P(("grp", "fsdp", "tp"), None),
            P(),
            P(("grp", "fsdp"), "tp"),
            P(("grp", "fsdp"), "tp"),
            P(("grp", "fsdp"), "tp"),
            P(("grp", "fsdp"), "tp"),
            P(("grp", "fsdp"), "tp"),
            P(("grp", "fsdp"), "tp"),
            P(("grp", "fsdp"), "tp"),
            P(),
            P(),
            P(),
            P(),
            P(),
            P(),
            P(("grp", "fsdp"), "tp"),
            P(),
            P(("grp", "fsdp"), "tp"),
            P(("grp", "fsdp"), "tp"),
            P(("grp", "fsdp"), "tp"),
        ),
        check_vma=False,
    )
```

profile of v0, /device:TPU:0, one launch (start us, length us, event | category | flops | bytes accessed | tf_op | source)
XLA Modules:
  0.0 848.1 jit_solution(16051372073277981679)
XLA Ops:
  11.5 12.8 %all_gather.56 = bf16[384,1024]{1,0:T(8,128)(2,1)S(1)} all-gather(bf16[192,1024]{1,0:T(8,128)(2,1)S(1)} %fusion.86), channel_id=1, replica_groups=mesh['grp'=4,'fsdp'=4,'tp'=2] {'tp'}, dimensions={0}, use_global_device_ids=true | all-gather | bytes 1179648 | tf_op jit(solution)/shard_map/all_gather | solution.py:214
  25.0 5.3 all_gather.62
  35.2 5.4 all_gather.57
  42.4 10.5 %all_gather.59 = bf16[1024,256]{1,0:T(8,128)(2,1)S(1)} all-gather(bf16[256,256]{1,0:T(8,128)(2,1)S(1)} %copy-done.88), channel_id=1, replica_groups=mesh['grp'=4,'fsdp'=4,'tp'=2] {'fsdp'}, dimensions={0}, use_global_device_ids=true | all-gather | bytes 655360 | tf_op jit(solution)/shard_map/all_gather | solution.py:148
  54.1 5.4 all_gather.58
  61.1 7.3 all_gather.60
  97.4 9.2 %while.34 = (s32[]{:T(128)}, f32[12,64,128]{2,1,0:T(8,128)S(1)}, f32[3,12,64,128]{3,2,1,0:T(8,128)S(1)}, f32[3,12,1,1]{1,3,2,0:T(1,128)}, f32[3,12]{1,0:T(4,128)...) while((s32[]{:T(128)}, f32[12,64,128]{2,1,0:T(8,128)S(1)}, ...), condition=%wide.region_5.6_spmd.clone, body=%wide.region_4.5_spmd.clone.sunk | while | flops 393219 | bytes 1967368 | solution.py:108
  109.9 5.9 fusion.27
  122.3 4.3 multiply_convert_fusion.3
  126.6 4.1 convolution_add_fusion.1
  133.9 17.4 %all_gather.69 = bf16[384,1024]{1,0:T(8,128)(2,1)} all-gather(bf16[192,1024]{1,0:T(8,128)(2,1)S(1)} %fusion.93), channel_id=1, replica_groups=mesh['grp'=4,'fsdp'=4,'tp'=2] {'tp'}, dimensions={0}, use_global_device_ids=true | all-gather | bytes 1179648 | tf_op jit(solution)/shard_map/all_gather | solution.py:215
  151.2 12.9 %reduce-scatter.11.cloned.1.call-done = f32[192,1024]{1,0:T(8,128)} async-done(((f32[384,1024]{1,0:T(8,128)}), f32[192,1024]{1,0:T(8,128)}) %reduce-scatter.11.cloned.1.call-update) | async-done | bytes 786448 | tf_op jit(solution)/shard_map/reduce_scatter | solution.py:276
  166.8 12.0 %all_gather.65 = bf16[384,1024]{1,0:T(8,128)(2,1)S(1)} all-gather(bf16[192,1024]{1,0:T(8,128)(2,1)S(1)} %multiply_convert_fusion.5), channel_id=1, replica_groups=mesh['grp'=4,'fsdp'=4,'tp'=2] {'tp'}, dimensions={0}, use_global_device_ids=true | all-gather | bytes 1179648 | tf_op jit(solution)/shard_map/all_gather | solution.py:280
  178.8 12.5 %all-gather.13.cloned.1.call-done = bf16[1024,1024]{1,0:T(8,128)(2,1)} async-done(((bf16[256,1024]{1,0:T(8,128)(2,1)}), bf16[1024,1024]{1,0:T(8,128)(2,1)}) %all-gather.13.cloned.1.call-update) | async-done | bytes 2097168 | tf_op jit(solution)/shard_map/all_gather | solution.py:148
  191.3 3.8 fusion.172
  195.0 20.3 %all-gather.15.cloned.1.call-done = bf16[1024,1024]{1,0:T(8,128)(2,1)} async-done(((bf16[256,1024]{1,0:T(8,128)(2,1)}), bf16[1024,1024]{1,0:T(8,128)(2,1)}) %all-gather.15.cloned.1.call-update) | async-done | bytes 2097168 | tf_op jit(solution)/shard_map/all_gather | solution.py:148
  219.1 20.5 %all-gather.17.cloned.1.call-done = bf16[1024,1024]{1,0:T(8,128)(2,1)} async-done(((bf16[256,1024]{1,0:T(8,128)(2,1)}), bf16[1024,1024]{1,0:T(8,128)(2,1)}) %all-gather.17.cloned.1.call-update) | async-done | bytes 2097168 | tf_op jit(solution)/shard_map/all_gather | solution.py:148
  239.6 5.2 multiply_convert_fusion
  254.0 21.5 %reduce-scatter.15.cloned.1.call-done = f32[192,1024]{1,0:T(8,128)} async-done(((f32[384,1024]{1,0:T(8,128)}), f32[192,1024]{1,0:T(8,128)}) %reduce-scatter.15.cloned.1.call-update) | async-done | bytes 786448 | tf_op jit(solution)/shard_map/reduce_scatter | solution.py:311
  278.2 17.0 %reduce-scatter.13.cloned.1.call-done = bf16[192,1024]{1,0:T(8,128)(2,1)} async-done(((bf16[384,1024]{1,0:T(8,128)(2,1)}), bf16[192,1024]{1,0:T(8,128)(2,1)}) %reduce-scatter.13.cloned.1.call-update) | async-done | bytes 393232 | tf_op jit(solution)/shard_map/reduce_scatter | solution.py:288
  298.3 11.5 %all_gather.70 = bf16[384,1024]{1,0:T(8,128)(2,1)S(1)} all-gather(bf16[192,1024]{1,0:T(8,128)(2,1)S(1)} %get-tuple-element.390), channel_id=1, replica_groups=mesh['grp'=4,'fsdp'=4,'tp'=2] {'tp'}, dimensions={0}, use_global_device_ids=true | all-gather | bytes 1179648 | tf_op jit(solution)/shard_map/all_gather | solution.py:320
  324.6 6.4 fusion.31
  332.2 8.4 while.35
  344.9 3.8 fusion.24
  404.3 5.6 pad_maximum_fusion
  409.9 12.7 %copy.226 = f32[1024,3072]{1,0:T(8,128)} copy(f32[1024,3072]{0,1:T(8,128)} %pad_maximum_fusion) | data formatting | bytes 25165824
  435.4 33.5 %concatenate.39 = f32[1024,2956]{0,1:T(8,128)} concatenate(f32[1024,256]{0,1:T(8,128)S(1)} %fusion.187, f32[1024,64]{0,1:T(8,128)S(1)} %copy-done.61, f32[1024,64]{0,1:T(8,128)} %fusion.188, f32[1024,256]{0,1:T(8,128)} %fusion.189, f32[1024,768]{0,1:T(8,128)} %fusion.180, f32[1024,768]{0,1:T(8,128)} %fusion.181, f32[1024,12]{0,1:T(8,128)S(1)} %fusion.136, f32[1024,768]{0,1:T(8,128)} %fusion.182), dimensions={1} | concatenate | bytes 24215552 | tf_op jit(solution)/shard_map/concatenate | solution.py:401
  468.9 12.6 %copy.224 = f32[1024,2956]{1,0:T(8,128)} copy(f32[1024,2956]{0,1:T(8,128)} %concatenate.39) | data formatting | bytes 24215552
  487.4 43.9 %all-reduce.20 = (f32[1024]{0:T(1024)}, f32[4,1536]{1,0:T(4,128)}, f32[4,256]{1,0:T(4,128)}, f32[24]{0:T(128)}, f32[24]{0:T(128)}, /*index=5*/f32[24]{0:T(128)}, f32[1024]{0:T(1024)}) all-reduce(f32[1024]{0:T(1024)S(1)} %get-tuple-element.339, ...), channel_id=1, replica_groups=mesh['grp'=4,'fsdp'=4,'tp'=2] {'grp','fsdp','tp'}, use_global_device_ids=true, to_apply=%region_25.26 | all-reduce | flops 9288 | bytes 74304 | tf_op jit(solution)/shard_map/psum | solution.py:436
  532.2 34.2 %reduce-scatter.21.cloned.1.call-done = f32[64,3072]{1,0:T(8,128)} async-done(((f32[1024,3072]{1,0:T(8,128)}), f32[64,3072]{1,0:T(8,128)}) %reduce-scatter.21.cloned.1.call-update) | async-done | bytes 786448
  568.5 135.9 %reduce-scatter.19.cloned.1.call-done = f32[64,2956]{1,0:T(8,128)} async-done(((f32[1024,2956]{1,0:T(8,128)}), f32[64,2956]{1,0:T(8,128)}) %reduce-scatter.19.cloned.1.call-update) | async-done | bytes 756752
  710.8 128.3 %all-reduce.23.cloned.1.call-done = f32[1024,256]{1,0:T(8,128)} async-done(((f32[1024,256]{1,0:T(8,128)}), f32[1024,256]{1,0:T(8,128)}) %all-reduce.23.cloned.1.call-update) | async-done | bytes 1048592 | tf_op jit(solution)/shard_map/psum | solution.py:436
  (539 shorter events, 198.4 us)
Async XLA Ops:
  7.2 61.2 %copy-start = (bf16[1024,256]{1,0:T(8,128)(2,1)S(1)}, bf16[1024,256]{1,0:T(8,128)(2,1)}, u32[]{:S(2)}) copy-start(bf16[1024,256]{1,0:T(8,128)(2,1)} %param.36) | copy-start | bytes 1572868
  7.2 76.4 %all-gather.7.cloned.1.call-start = ((), (), s32[]{:S(2)}) async-start(), calls=%async_computation.6 | async-start | bytes 1966080 | tf_op jit(solution)/shard_map/all_gather | solution.py:148
  8.0 17.0 %copy-start.145 = (bf16[256,12]{0,1:T(8,128)(2,1)S(1)}, bf16[256,12]{0,1:T(8,128)(2,1)}, u32[]{:S(2)}) copy-start(bf16[256,12]{0,1:T(8,128)(2,1)} %param.35) | copy-start | bytes 18436
  8.0 22.4 %copy-start.162 = (f32[24]{0:T(128)S(1)}, f32[24]{0:T(128)}, u32[]{:S(2)}) copy-start(f32[24]{0:T(128)} %param.40) | copy-start | bytes 292
  8.0 114.3 %all-gather.9.cloned.1.call-start = ((), (), s32[]{:S(2)}) async-start(), calls=%async_computation.7 | async-start | bytes 1966080 | tf_op jit(solution)/shard_map/all_gather | solution.py:148
  8.7 117.8 %all-gather.11.cloned.1.call-start = ((), (), s32[]{:S(2)}) async-start(), calls=%async_computation.8 | async-start | bytes 1966080 | tf_op jit(solution)/shard_map/all_gather | solution.py:148
  9.5 154.7 %reduce-scatter.11.cloned.1.call-start = ((), (), s32[]{:S(2)}) async-start(), calls=%async_computation.9 | async-start | bytes 2359296 | tf_op jit(solution)/shard_map/reduce_scatter | solution.py:276
  9.5 50.6 %copy-start.148 = (f32[32]{0:T(128)}, f32[32]{0:T(128)S(1)}, u32[]{:S(2)}) copy-start(f32[32]{0:T(128)S(1)} %multiply_power_fusion) | copy-start | bytes 388
  9.5 50.6 %copy-start.108 = (f32[384]{0:T(512)}, f32[384]{0:T(512)S(1)}, u32[]{:S(2)}) copy-start(f32[384]{0:T(512)S(1)} %iota_convert_fusion) | copy-start | bytes 4612
  11.4 20.1 %copy-start.159 = (f32[24]{0:T(128)S(1)}, f32[24]{0:T(128)}, u32[]{:S(2)}) copy-start(f32[24]{0:T(128)} %param.39) | copy-start | bytes 292
  11.5 23.7 %copy-start.110 = (bf16[256,64]{0,1:T(8,128)(2,1)S(1)}, bf16[256,64]{0,1:T(8,128)(2,1)}, u32[]{:S(2)}) copy-start(bf16[256,64]{0,1:T(8,128)(2,1)} %param.31) | copy-start | bytes 98308
  25.0 16.6 %copy-start.112 = (f32[384]{0:T(512)}, f32[384]{0:T(512)S(1)}, u32[]{:S(2)}) copy-start(f32[384]{0:T(512)S(1)} %fusion.149) | copy-start | bytes 4612
  31.5 38.4 %copy-start.38 = (f32[3,128,12]{2,1,0:T(8,128)}, f32[3,128,12]{2,1,0:T(8,128)S(1)}, u32[]{:S(2)}) copy-start(f32[3,128,12]{2,1,0:T(8,128)S(1)} %copy.164) | copy-start | bytes 55300
  32.7 21.4 %copy-start.125 = (f32[3,1,12]{2,1,0:T(1,128)}, f32[3,1,12]{2,1,0:T(1,128)S(1)}, u32[]{:S(2)}) copy-start(f32[3,1,12]{2,1,0:T(1,128)S(1)} %slice.153) | copy-start | bytes 436
  33.3 36.7 %copy-start.107 = (f32[3,1,12]{2,0,1:T(4,128)}, f32[3,1,12]{2,0,1:T(4,128)S(1)}, u32[]{:S(2)}) copy-start(f32[3,1,12]{2,0,1:T(4,128)S(1)} %copy.277) | copy-start | bytes 436
  52.9 15.5 %copy-start.156 = (f32[4,256]{1,0:T(4,128)S(1)}, f32[4,256]{1,0:T(4,128)}, u32[]{:S(2)}) copy-start(f32[4,256]{1,0:T(4,128)} %param.38) | copy-start | bytes 12292
  69.9 23.8 %copy-start.19 = (f32[384,128]{1,0:T(8,128)}, f32[384,128]{1,0:T(8,128)S(1)}, u32[]{:S(2)}) copy-start(f32[384,128]{1,0:T(8,128)S(1)} %get-tuple-element.425) | copy-start | bytes 589828
  71.8 21.9 %copy-start.77 = (f32[3,128,12]{1,2,0:T(8,128)}, f32[3,128,12]{1,2,0:T(8,128)S(1)}, u32[]{:S(2)}) copy-start(f32[3,128,12]{1,2,0:T(8,128)S(1)} %copy.170) | copy-start | bytes 55300
  130.7 60.6 %all-gather.13.cloned.1.call-start = ((), (), s32[]{:S(2)}) async-start(), calls=%async_computation.10 | async-start | bytes 2621440 | tf_op jit(solution)/shard_map/all_gather | solution.py:148
  131.3 84.1 %all-gather.15.cloned.1.call-start = ((), (), s32[]{:S(2)}) async-start(), calls=%async_computation.11 | async-start | bytes 2621440 | tf_op jit(solution)/shard_map/all_gather | solution.py:148
  131.8 107.8 %all-gather.17.cloned.1.call-start = ((), (), s32[]{:S(2)}) async-start(), calls=%async_computation.12 | async-start | bytes 2621440 | tf_op jit(solution)/shard_map/all_gather | solution.py:148
  132.6 142.9 %reduce-scatter.15.cloned.1.call-start = ((), (), s32[]{:S(2)}) async-start(), calls=%async_computation.14 | async-start | bytes 2359296 | tf_op jit(solution)/shard_map/reduce_scatter | solution.py:311
  178.8 36.6 %copy-start.8 = (bf16[384,1024]{1,0:T(8,128)(2,1)}, bf16[384,1024]{1,0:T(8,128)(2,1)S(1)}, u32[]{:S(2)}) copy-start(bf16[384,1024]{1,0:T(8,128)(2,1)S(1)} %all_gather.65) | copy-start | bytes 2359300
  249.3 46.0 %reduce-scatter.13.cloned.1.call-start = ((), (), s32[]{:S(2)}) async-start(), calls=%async_computation.13 | async-start | bytes 1179648 | tf_op jit(solution)/shard_map/reduce_scatter | solution.py:288
  253.9 41.4 %copy-start.53 = (bf16[192,1024]{1,0:T(8,128)(2,1)S(1)}, bf16[192,1024]{1,0:T(8,128)(2,1)}, u32[]{:S(2)}) copy-start(bf16[192,1024]{1,0:T(8,128)(2,1)} %param.47) | copy-start | bytes 1179652
  253.9 231.9 %reduce-scatter.17.cloned.1.call-start = ((), (), s32[]{:S(2)}) async-start(), calls=%async_computation.15 | async-start | bytes 2359296 | tf_op jit(solution)/shard_map/reduce_scatter | solution.py:390
  398.8 167.7 %reduce-scatter.21.cloned.1.call-start = ((), (), s32[]{:S(2)}) async-start(), calls=%async_computation.18 | async-start | bytes 13369344
  422.7 281.7 %reduce-scatter.19.cloned.1.call-start = ((), (), s32[]{:S(2)}) async-start(), calls=%async_computation.17 | async-start | bytes 13369344
  481.6 357.5 %all-reduce.23.cloned.1.call-start = ((), (), s32[]{:S(2)}) async-start(), calls=%async_computation.16 | async-start | bytes 2097152 | tf_op jit(solution)/shard_map/psum | solution.py:436
  485.7 45.5 %copy-start.39 = (f32[192,1024]{1,0:T(8,128)S(1)}, f32[192,1024]{1,0:T(8,128)}, u32[]{:S(2)}) copy-start(f32[192,1024]{1,0:T(8,128)} %get-tuple-element.391) | copy-start | bytes 2359300
  485.7 45.5 %copy-start.150 = (f32[192]{0:T(256)S(1)}, f32[192]{0:T(256)}, u32[]{:S(2)}) copy-start(f32[192]{0:T(256)} %get-tuple-element.439) | copy-start | bytes 2308
  485.9 45.3 %copy-start.37 = (f32[192,1024]{1,0:T(8,128)S(1)}, f32[192,1024]{1,0:T(8,128)}, u32[]{:S(2)}) copy-start(f32[192,1024]{1,0:T(8,128)} %reduce-scatter.17.cloned.1.call-done) | copy-start | bytes 2359300
  (145 other events, 476.4 us)
Sparse Core Ops, SparseCore 0:
  9.6 22.5 all-gather.6
  33.7 22.4 all-gather.8
  57.8 19.6 all-gather.10
  130.8 33.2 reduce-scatter.10
  165.6 25.6 all-gather.12
  192.8 22.5 all-gather.14
  217.0 22.5 all-gather.16
  249.4 26.0 reduce-scatter.14
  277.8 17.4 reduce-scatter.12
  398.9 26.1 reduce-scatter.16
  429.1 137.2 reduce-scatter.20
  570.4 133.9 reduce-scatter.18
  710.1 128.9 all-reduce.22
where the time goes:
time: 859 us; the launch traced here: 848 us
  waiting for transfers between devices  407 us (47%)
  blocking collectives  131 us (15%)
  local copies, waits for them, and re-layouts  128 us (15%)
  matrix products  108 us (13%)
  other arithmetic  55.6 us (6%)
  between operations  16.6 us (2%)
    unnamed x15, waiting for transfers between devices  174 us
    psum x1, waiting for transfers between devices, local(): lax.psum((gain1_part, shared_w_grad, kernel_full, conv_shared_grad, decay...  128 us
    all_gather x6, waiting for transfers between devices, gather_weights(): lax.all_gather(for_sending(weights), 'fsdp', axis=0, tiled=True)  53.4 us
    psum x1, blocking collectives, local(): lax.psum((gain1_part, shared_w_grad, kernel_full, conv_shared_grad, decay...  43.9 us
    unnamed x333, local copies, waits for them, and re-layouts  41 us
    all_gather x5, blocking collectives, gather_weights(): lax.all_gather(for_sending(weights), 'fsdp', axis=0, tiled=True)  33.9 us
    concatenate x1, local copies, waits for them, and re-layouts, mixer_terms(): jnp.concatenate([dot_tn(normed1_all, query_back), dot_tn(normed1_all, key...  33.5 us
    reduce_scatter x1, waiting for transfers between devices, local(): lax.psum_scatter(norm2_part, 'tp', scatter_dimension=0, tiled=True)  21.5 us
  transfers between devices with their start and end apart: 13, of which 9 were waited for; matrix products, arithmetic and copies ran while one was open for 21% of the time, Pallas kernels for 0%

commit v1 on v0

--- a/solution.py
+++ b/solution.py
@@ -89,8 +89,9 @@
     step_blk = step_sizes.reshape(blocks, BLOCK, head_count)
     b_blk = b_matrix.reshape(blocks, BLOCK, nstate)
     c_blk = c_matrix.reshape(blocks, BLOCK, nstate)
-    cumulative = jnp.cumsum(step_blk * rates, axis=1)
     index_t = jnp.arange(BLOCK)
+    lower = (index_t[:, None] >= index_t[None, :]).astype(jnp.float32)
+    cumulative = jnp.einsum("ts,csh->cth", lower, step_blk * rates, precision=top_precision)
     causal = (index_t[:, None] >= index_t[None, :])[None, :, :, None]
     log_gaps = cumulative[:, :, None, :] - cumulative[:, None, :, :]
     decay_mat = jnp.where(causal, jnp.exp(jnp.where(causal, log_gaps, 0.0)), 0.0)
@@ -150,26 +151,13 @@
     )
 
 
-def gather_again(weights):
-    return jax.tree.map(
-        lambda part, own: part.astype(own.dtype),
-        lax.all_gather(for_sending(weights), "fsdp", axis=0, tiled=True),
-        weights,
-    )
-
-
-def reduce_weight_grads(term_fn, model_width):
-    group_count = lax.axis_size("grp")
-    fsdp_count = lax.axis_size("fsdp")
-    return lax.psum_scatter(
-        term_fn(
-            jnp.int32(0),
-            lax.axis_size(("grp", "fsdp")) * (model_width // (group_count * fsdp_count)),
-        ),
-        ("grp", "fsdp"),
-        scatter_dimension=0,
-        tiled=True,
-    )
+def reduce_weight_grads(terms):
+    return [
+        lax.psum_scatter(
+            term.astype(jnp.bfloat16), ("grp", "fsdp"), scatter_dimension=0, tiled=True
+        ).astype(jnp.float32)
+        for term in terms
+    ]
 
 
 def local(
@@ -289,24 +277,20 @@
         ffn_part.astype(jnp.bfloat16), "tp", scatter_dimension=0, tiled=True
     ).astype(jnp.float32)
     output = ((resid_mid + ffn_sum) * valid_own).astype(jnp.bfloat16)
-    ffn_back = gather_again((w_ffn_gate, w_ffn_up, w_ffn_down))
+    ffn_back = ffn_full
     wg_back, wu_back, wd_back = ffn_back
     hidden_grad = jnp.dot(top_grad_all, wd_back, preferred_element_type=jnp.float32)
     silu_slope = sigma_gate * (1.0 + gate_pre * (1.0 - sigma_gate))
     gate_grad = (hidden_grad * up_pre * silu_slope).astype(jnp.bfloat16)
     up_grad = (hidden_grad * silu_gate).astype(jnp.bfloat16)
 
-    def ffn_terms(start, count):
-        return jnp.concatenate(
-            [
-                dot_tn(normed2_all, gate_grad),
-                dot_tn(normed2_all, up_grad),
-                dot_tn(top_grad_all, hidden_low),
-            ],
-            axis=1,
-        )
-
-    ffn_grads = reduce_weight_grads(ffn_terms, model_width)
+    ffn_grads = reduce_weight_grads(
+        [
+            dot_tn(normed2_all, gate_grad),
+            dot_tn(normed2_all, up_grad),
+            dot_tn(top_grad_all, hidden_low),
+        ]
+    )
     norm2_part = dot_nt(gate_grad, wg_back) + dot_nt(up_grad, wu_back)
     norm2_grad = lax.psum_scatter(norm2_part, "tp", scatter_dimension=0, tiled=True)
     gain2_part = jnp.sum(norm2_grad * resid_mid * scale_two, axis=0)
@@ -318,9 +302,7 @@
     )
     mix_grad_low = resid_grad.astype(jnp.bfloat16)
     mix_grad_all = lax.all_gather(mix_grad_low, "tp", axis=0, tiled=True)
-    mixer_back = gather_again(
-        (w_query, key_weight, value_weight, w_attn_out, w_mamba_z, w_mamba_x, w_step, w_mamba_out)
-    )
+    mixer_back = mixer_full
     wq_back, wk_back, wv_back, wo_back, wz_back, wx_back, wdt_back, wout_back = mixer_back
     attn_grad = jnp.dot(mix_grad_all, wo_back, preferred_element_type=jnp.float32).astype(
         jnp.bfloat16
@@ -397,22 +379,18 @@
     )
     grad_in = input_grad.astype(jnp.bfloat16)
 
-    def mixer_terms(start, count):
-        return jnp.concatenate(
-            [
-                dot_tn(normed1_all, query_back),
-                dot_tn(normed1_all, key_back),
-                dot_tn(normed1_all, value_back),
-                dot_tn(mix_grad_all, attn_low),
-                dot_tn(normed1_all, gate_back_low),
-                dot_tn(normed1_all, main_back_low),
-                dot_tn(normed1_all, step_back_low),
-                dot_tn(mix_grad_all, mamba_low),
-            ],
-            axis=1,
-        )
-
-    mixer_grads = reduce_weight_grads(mixer_terms, model_width)
+    mixer_parts = reduce_weight_grads(
+        [
+            dot_tn(normed1_all, query_back),
+            dot_tn(normed1_all, key_back),
+            dot_tn(normed1_all, value_back),
+            dot_tn(mix_grad_all, attn_low),
+            dot_tn(normed1_all, gate_back_low),
+            dot_tn(normed1_all, main_back_low),
+            dot_tn(normed1_all, step_back_low),
+            dot_tn(mix_grad_all, mamba_low),
+        ]
+    )
     shared_w_grad = lax.dot_general(
         normed1_all.astype(jnp.float32),
         shared_back,
@@ -447,22 +425,6 @@
             ("grp", "fsdp", "tp"),
         )
     )
-    mixer_widths = [
-        wq_all.shape[1],
-        wk_all.shape[1],
-        wv_all.shape[1],
-        wo_all.shape[1],
-        wz_all.shape[1],
-        wx_all.shape[1],
-        wdt_all.shape[1],
-        wout_all.shape[1],
-    ]
-    mixer_parts = []
-    column = 0
-    for width_now in mixer_widths:
-        mixer_parts.append(mixer_grads[:, column : column + width_now])
-        column = column + width_now
-    ffn_width = wg_all.shape[1]
     return (
         output,
         grad_in,
@@ -482,9 +444,9 @@
         skip_sum,
         mixer_parts[7],
         gain2_sum,
-        ffn_grads[:, :ffn_width],
-        ffn_grads[:, ffn_width : 2 * ffn_width],
-        ffn_grads[:, 2 * ffn_width :],
+        ffn_grads[0],
+        ffn_grads[1],
+        ffn_grads[2],
     )
 
 

time: 859 us -> 1140 us (1.33)
  waiting for transfers between devices: 407 us -> 740 us
  local copies, waits for them, and re-layouts: 128 us -> 54.4 us
  matrix products: 108 us -> 126 us
    reduce_scatter x0 -> x10, waiting for transfers between devices: none -> 467 us  [reduce_weight_grads(): lax.psum_scatter(term.astype(jnp.bfloat16), ('grp', 'fsdp'), scatter_dime...]
    unnamed x15 -> x23, waiting for transfers between devices: 174 us -> 60.3 us
    psum x1, waiting for transfers between devices: 128 us -> 92.5 us  [local(): lax.psum((gain1_part, shared_w_grad, kernel_full, conv_shared_grad, decay...]
    concatenate x1 -> x0, local copies, waits for them, and re-layouts: 33.5 us -> none  [mixer_terms(): jnp.concatenate([dot_tn(normed1_all, query_back), dot_tn(normed1_all, key...]
    unnamed x333 -> x283, local copies, waits for them, and re-layouts: 41 us -> 14.1 us
    reduce_scatter x1, waiting for transfers between devices: 0.02 us -> 25.9 us  [local(): lax.psum_scatter(norm1_part, 'tp', scatter_dimension=0, tiled=True)]
    convert_element_type x0 -> x11, other arithmetic: none -> 15.8 us  [reduce_weight_grads(): return [lax.psum_scatter(term.astype(jnp.bfloat16), ('grp', 'fsdp'), scat...]
  transfers between devices with their start and end apart: 13 -> 22, of which waited for: 9 -> 17; matrix products, arithmetic and copies ran while one was open for 21% -> 19% of each run, Pallas kernels for 0% -> 0%
where the time goes in v1:
time: 1140 us; the launch traced here: 1130 us
  waiting for transfers between devices  740 us (65%)
  blocking collectives  128 us (11%)
  matrix products  126 us (11%)
  other arithmetic  63.4 us (6%)
  local copies, waits for them, and re-layouts  54.4 us (5%)
  between operations  17.2 us (2%)
    reduce_scatter x10, waiting for transfers between devices, reduce_weight_grads(): lax.psum_scatter(term.astype(jnp.bfloat16), ('grp', 'fsdp'), scatter_dime...  467 us
    psum x1, waiting for transfers between devices, local(): lax.psum((gain1_part, shared_w_grad, kernel_full, conv_shared_grad, decay...  92.5 us
    unnamed x23, waiting for transfers between devices  60.3 us
    all_gather x6, waiting for transfers between devices, gather_weights(): lax.all_gather(for_sending(weights), 'fsdp', axis=0, tiled=True)  52.8 us
    psum x1, blocking collectives, local(): lax.psum((gain1_part, shared_w_grad, kernel_full, conv_shared_grad, decay...  40.9 us
    all_gather x5, blocking collectives, gather_weights(): lax.all_gather(for_sending(weights), 'fsdp', axis=0, tiled=True)  34 us
    dot_general x11, matrix products, dot_tn(): lax.dot_general(first_mat, second_mat, (((0,), (0,)), ((), ())), preferre...  27.1 us
    reduce_scatter x1, waiting for transfers between devices, local(): lax.psum_scatter(norm1_part, 'tp', scatter_dimension=0, tiled=True)  25.9 us
  transfers between devices with their start and end apart: 22, of which 17 were waited for; matrix products, arithmetic and copies ran while one was open for 19% of the time, Pallas kernels for 0%

profile of v1, /device:TPU:0, one launch (start us, length us, event | category | flops | bytes accessed | tf_op | source)
XLA Modules:
  0.0 1130.4 jit_solution(15644586802818256261)
XLA Ops:
  11.4 12.8 %all_gather.45 = bf16[384,1024]{1,0:T(8,128)(2,1)S(1)} all-gather(bf16[192,1024]{1,0:T(8,128)(2,1)S(1)} %fusion.86), channel_id=1, replica_groups=mesh['grp'=4,'fsdp'=4,'tp'=2] {'tp'}, dimensions={0}, use_global_device_ids=true | all-gather | bytes 1179648 | tf_op jit(solution)/shard_map/all_gather | solution.py:202
  24.9 5.3 all_gather.51
  36.6 7.3 all_gather.48
  44.4 7.5 all_gather.47
  54.2 5.4 all_gather.46
  60.6 8.4 all_gather.49
  89.8 9.2 while.34
  101.3 5.9 fusion.27
  124.6 16.3 %all_gather.58 = bf16[384,1024]{1,0:T(8,128)(2,1)} all-gather(bf16[192,1024]{1,0:T(8,128)(2,1)S(1)} %fusion.93), channel_id=1, replica_groups=mesh['grp'=4,'fsdp'=4,'tp'=2] {'tp'}, dimensions={0}, use_global_device_ids=true | all-gather | bytes 1179648 | tf_op jit(solution)/shard_map/all_gather | solution.py:203
  140.9 14.0 %reduce-scatter.18.cloned.1.call-done = f32[192,1024]{1,0:T(8,128)} async-done(((f32[384,1024]{1,0:T(8,128)}), f32[192,1024]{1,0:T(8,128)}) %reduce-scatter.18.cloned.1.call-update) | async-done | bytes 786448 | tf_op jit(solution)/shard_map/reduce_scatter | solution.py:264
  157.4 12.2 %all_gather.54 = bf16[384,1024]{1,0:T(8,128)(2,1)} all-gather(bf16[192,1024]{1,0:T(8,128)(2,1)S(1)} %multiply_convert_fusion.5), channel_id=1, replica_groups=mesh['grp'=4,'fsdp'=4,'tp'=2] {'tp'}, dimensions={0}, use_global_device_ids=true | all-gather | bytes 1179648 | tf_op jit(solution)/shard_map/all_gather | solution.py:268
  169.6 12.4 %all-gather.13.cloned.1.call-done = bf16[1024,1024]{1,0:T(8,128)(2,1)} async-done(((bf16[256,1024]{1,0:T(8,128)(2,1)}), bf16[1024,1024]{1,0:T(8,128)(2,1)}) %all-gather.13.cloned.1.call-update) | async-done | bytes 2097168 | tf_op jit(solution)/shard_map/all_gather | solution.py:149
  186.0 20.1 %all-gather.15.cloned.1.call-done = bf16[1024,1024]{1,0:T(8,128)(2,1)} async-done(((bf16[256,1024]{1,0:T(8,128)(2,1)}), bf16[1024,1024]{1,0:T(8,128)(2,1)}) %all-gather.15.cloned.1.call-update) | async-done | bytes 2097168 | tf_op jit(solution)/shard_map/all_gather | solution.py:149
  210.1 20.3 %all-gather.17.cloned.1.call-done = bf16[1024,1024]{1,0:T(8,128)(2,1)} async-done(((bf16[256,1024]{1,0:T(8,128)(2,1)}), bf16[1024,1024]{1,0:T(8,128)(2,1)}) %all-gather.17.cloned.1.call-update) | async-done | bytes 2097168 | tf_op jit(solution)/shard_map/all_gather | solution.py:149
  256.1 10.2 reduce-scatter.22.cloned.1.call-done
  269.0 17.0 %reduce-scatter.20.cloned.1.call-done = bf16[192,1024]{1,0:T(8,128)(2,1)} async-done(((bf16[384,1024]{1,0:T(8,128)(2,1)}), bf16[192,1024]{1,0:T(8,128)(2,1)}) %reduce-scatter.20.cloned.1.call-update) | async-done | bytes 393232 | tf_op jit(solution)/shard_map/reduce_scatter | solution.py:276
  289.1 11.5 %all_gather.59 = bf16[384,1024]{1,0:T(8,128)(2,1)S(1)} all-gather(bf16[192,1024]{1,0:T(8,128)(2,1)S(1)} %get-tuple-element.304), channel_id=1, replica_groups=mesh['grp'=4,'fsdp'=4,'tp'=2] {'tp'}, dimensions={0}, use_global_device_ids=true | all-gather | bytes 1179648 | tf_op jit(solution)/shard_map/all_gather | solution.py:304
  315.6 6.5 fusion.31
  323.9 11.4 %while.35 = (s32[]{:T(128)}, f32[12,64,128]{2,1,0:T(8,128)S(1)}, f32[3,12]{1,0:T(4,128)}, f32[3,12,64,128]{3,2,1,0:T(8,128)}, f32[3,12,64,128]{3,2,1,0:T(8,128)}...) while((s32[]{:T(128)}, f32[12,64,128]{2,1,0:T(8,128)S(1)}, ...), condition=%wide.region_13.14_spmd.clone, body=%wide.region_11.13_spmd.clone.sunk | while | flops 589816 | bytes 2359724 | solution.py:109
  372.4 5.6 fusion.24
  422.3 58.2 %reduce-scatter.44.cloned.1.call-done = bf16[64,1024]{1,0:T(8,128)(2,1)} async-done(((bf16[1024,1024]{1,0:T(8,128)(2,1)}), bf16[64,1024]{1,0:T(8,128)(2,1)}) %reduce-scatter.44.cloned.1.call-update) | async-done | bytes 131088 | tf_op jit(solution)/shard_map/reduce_scatter | solution.py:156
  482.2 56.2 %reduce-scatter.46.cloned.1.call-done = bf16[64,12]{1,0:T(8,128)(2,1)} async-done(((bf16[1024,12]{1,0:T(8,128)(2,1)}), bf16[64,12]{1,0:T(8,128)(2,1)}) %reduce-scatter.46.cloned.1.call-update) | async-done | bytes 1552
  539.8 56.3 %reduce-scatter.28.cloned.1.call-done = bf16[64,64]{1,0:T(8,128)(2,1)} async-done(((bf16[1024,64]{1,0:T(8,128)(2,1)}), bf16[64,64]{1,0:T(8,128)(2,1)}) %reduce-scatter.28.cloned.1.call-update) | async-done | bytes 8208 | tf_op jit(solution)/shard_map/reduce_scatter | solution.py:156
  597.5 56.4 %reduce-scatter.30.cloned.1.call-done = bf16[64,64]{1,0:T(8,128)(2,1)} async-done(((bf16[1024,64]{1,0:T(8,128)(2,1)}), bf16[64,64]{1,0:T(8,128)(2,1)}) %reduce-scatter.30.cloned.1.call-update) | async-done | bytes 8208 | tf_op jit(solution)/shard_map/reduce_scatter | solution.py:156
  655.2 56.9 %reduce-scatter.26.cloned.1.call-done = bf16[64,256]{1,0:T(8,128)(2,1)} async-done(((bf16[1024,256]{1,0:T(8,128)(2,1)}), bf16[64,256]{1,0:T(8,128)(2,1)}) %reduce-scatter.26.cloned.1.call-update) | async-done | bytes 32784 | tf_op jit(solution)/shard_map/reduce_scatter | solution.py:156
  713.5 57.2 %reduce-scatter.32.cloned.1.call-done = bf16[64,256]{1,0:T(8,128)(2,1)} async-done(((bf16[1024,256]{1,0:T(8,128)(2,1)}), bf16[64,256]{1,0:T(8,128)(2,1)}) %reduce-scatter.32.cloned.1.call-update) | async-done | bytes 32784 | tf_op jit(solution)/shard_map/reduce_scatter | solution.py:156
  772.1 60.7 %reduce-scatter.38.cloned.1.call-done = bf16[64,768]{1,0:T(8,128)(2,1)} async-done(((bf16[1024,768]{1,0:T(8,128)(2,1)}), bf16[64,768]{1,0:T(8,128)(2,1)}) %reduce-scatter.38.cloned.1.call-update) | async-done | bytes 98320 | tf_op jit(solution)/shard_map/reduce_scatter | solution.py:156
  834.4 61.1 %reduce-scatter.36.cloned.1.call-done = bf16[64,768]{1,0:T(8,128)(2,1)} async-done(((bf16[1024,768]{1,0:T(8,128)(2,1)}), bf16[64,768]{1,0:T(8,128)(2,1)}) %reduce-scatter.36.cloned.1.call-update) | async-done | bytes 98320 | tf_op jit(solution)/shard_map/reduce_scatter | solution.py:156
  897.1 60.4 %reduce-scatter.34.cloned.1.call-done = bf16[64,768]{1,0:T(8,128)(2,1)} async-done(((bf16[1024,768]{1,0:T(8,128)(2,1)}), bf16[64,768]{1,0:T(8,128)(2,1)}) %reduce-scatter.34.cloned.1.call-update) | async-done | bytes 98320 | tf_op jit(solution)/shard_map/reduce_scatter | solution.py:156
  959.0 25.9 %reduce-scatter.24.cloned.1.call-done = f32[192,1024]{1,0:T(8,128)} async-done(((f32[384,1024]{1,0:T(8,128)}), f32[192,1024]{1,0:T(8,128)}) %reduce-scatter.24.cloned.1.call-update) | async-done | bytes 786448 | tf_op jit(solution)/shard_map/reduce_scatter | solution.py:372
  986.4 40.9 %all-reduce.20 = (f32[1024]{0:T(1024)}, f32[4,1536]{1,0:T(4,128)}, f32[4,256]{1,0:T(4,128)}, f32[24]{0:T(128)}, f32[24]{0:T(128)}, /*index=5*/f32[24]{0:T(128)}, f32[1024]{0:T(1024)}) all-reduce(f32[1024]{0:T(1024)S(1)} %get-tuple-element.255, ...), channel_id=1, replica_groups=mesh['grp'=4,'fsdp'=4,'tp'=2] {'grp','fsdp','tp'}, use_global_device_ids=true, to_apply=%region_23.24 | all-reduce | flops 9288 | bytes 74304 | tf_op jit(solution)/shard_map/psum | solution.py:414
  1028.3 92.5 %all-reduce.23.cloned.1.call-done = f32[1024,256]{1,0:T(8,128)} async-done(((f32[1024,256]{1,0:T(8,128)}), f32[1024,256]{1,0:T(8,128)}) %all-reduce.23.cloned.1.call-update) | async-done | bytes 1048592 | tf_op jit(solution)/shard_map/psum | solution.py:414
  (505 shorter events, 231.9 us)
Async XLA Ops:
  7.2 27.0 %copy-start = (bf16[1024,256]{1,0:T(8,128)(2,1)S(1)}, bf16[1024,256]{1,0:T(8,128)(2,1)}, u32[]{:S(2)}) copy-start(bf16[1024,256]{1,0:T(8,128)(2,1)} %param.36) | copy-start | bytes 1572868
  7.2 68.8 %all-gather.7.cloned.1.call-start = ((), (), s32[]{:S(2)}) async-start(), calls=%async_computation.15 | async-start | bytes 1966080 | tf_op jit(solution)/shard_map/all_gather | solution.py:149
  8.0 105.6 %all-gather.9.cloned.1.call-start = ((), (), s32[]{:S(2)}) async-start(), calls=%async_computation.16 | async-start | bytes 1966080 | tf_op jit(solution)/shard_map/all_gather | solution.py:149
  8.7 109.2 %all-gather.11.cloned.1.call-start = ((), (), s32[]{:S(2)}) async-start(), calls=%async_computation.17 | async-start | bytes 1966080 | tf_op jit(solution)/shard_map/all_gather | solution.py:149
  9.5 145.4 %reduce-scatter.18.cloned.1.call-start = ((), (), s32[]{:S(2)}) async-start(), calls=%async_computation.18 | async-start | bytes 2359296 | tf_op jit(solution)/shard_map/reduce_scatter | solution.py:264
  24.9 99.0 %copy-start.92 = (f32[384]{0:T(512)}, f32[384]{0:T(512)S(1)}, u32[]{:S(2)}) copy-start(f32[384]{0:T(512)S(1)} %fusion.162) | copy-start | bytes 4612
  35.7 50.4 %copy-start.11 = (f32[384,128]{1,0:T(8,128)}, f32[384,128]{1,0:T(8,128)S(1)}, u32[]{:S(2)}) copy-start(f32[384,128]{1,0:T(8,128)S(1)} %get-tuple-element.329) | copy-start | bytes 589828
  122.0 60.1 %all-gather.13.cloned.1.call-start = ((), (), s32[]{:S(2)}) async-start(), calls=%async_computation.19 | async-start | bytes 2621440 | tf_op jit(solution)/shard_map/all_gather | solution.py:149
  122.5 83.6 %all-gather.15.cloned.1.call-start = ((), (), s32[]{:S(2)}) async-start(), calls=%async_computation.20 | async-start | bytes 2621440 | tf_op jit(solution)/shard_map/all_gather | solution.py:149
  123.1 107.3 %all-gather.17.cloned.1.call-start = ((), (), s32[]{:S(2)}) async-start(), calls=%async_computation.21 | async-start | bytes 2621440 | tf_op jit(solution)/shard_map/all_gather | solution.py:149
  123.9 142.4 %reduce-scatter.22.cloned.1.call-start = ((), (), s32[]{:S(2)}) async-start(), calls=%async_computation.23 | async-start | bytes 2359296 | tf_op jit(solution)/shard_map/reduce_scatter | solution.py:295
  124.6 32.5 %copy-start.81 = (f32[1024]{0:T(1024)S(1)}, f32[1024]{0:T(1024)}, u32[]{:S(2)}) copy-start(f32[1024]{0:T(1024)} %param.43) | copy-start | bytes 12292
  240.0 45.9 %reduce-scatter.20.cloned.1.call-start = ((), (), s32[]{:S(2)}) async-start(), calls=%async_computation.22 | async-start | bytes 1179648 | tf_op jit(solution)/shard_map/reduce_scatter | solution.py:276
  243.9 175.1 %reduce-scatter.40.cloned.1.call-start = ((), (), s32[]{:S(2)}) async-start(), calls=%async_computation.33 | async-start | bytes 2228224 | tf_op jit(solution)/shard_map/reduce_scatter | solution.py:156
  247.9 172.7 %reduce-scatter.42.cloned.1.call-start = ((), (), s32[]{:S(2)}) async-start(), calls=%async_computation.34 | async-start | bytes 2228224 | tf_op jit(solution)/shard_map/reduce_scatter | solution.py:156
  252.0 228.6 %reduce-scatter.44.cloned.1.call-start = ((), (), s32[]{:S(2)}) async-start(), calls=%async_computation.35 | async-start | bytes 2228224 | tf_op jit(solution)/shard_map/reduce_scatter | solution.py:156
  256.0 282.3 %reduce-scatter.46.cloned.1.call-start = ((), (), s32[]{:S(2)}) async-start(), calls=%async_computation.36 | async-start | bytes 278528
  359.8 236.3 %reduce-scatter.28.cloned.1.call-start = ((), (), s32[]{:S(2)}) async-start(), calls=%async_computation.26 | async-start | bytes 278528 | tf_op jit(solution)/shard_map/reduce_scatter | solution.py:156
  361.4 292.5 %reduce-scatter.30.cloned.1.call-start = ((), (), s32[]{:S(2)}) async-start(), calls=%async_computation.27 | async-start | bytes 278528 | tf_op jit(solution)/shard_map/reduce_scatter | solution.py:156
  364.7 347.4 %reduce-scatter.26.cloned.1.call-start = ((), (), s32[]{:S(2)}) async-start(), calls=%async_computation.25 | async-start | bytes 557056 | tf_op jit(solution)/shard_map/reduce_scatter | solution.py:156
  366.1 404.6 %reduce-scatter.32.cloned.1.call-start = ((), (), s32[]{:S(2)}) async-start(), calls=%async_computation.28 | async-start | bytes 557056 | tf_op jit(solution)/shard_map/reduce_scatter | solution.py:156
  368.6 464.2 %reduce-scatter.38.cloned.1.call-start = ((), (), s32[]{:S(2)}) async-start(), calls=%async_computation.32 | async-start | bytes 1671168 | tf_op jit(solution)/shard_map/reduce_scatter | solution.py:156
  372.3 523.2 %reduce-scatter.36.cloned.1.call-start = ((), (), s32[]{:S(2)}) async-start(), calls=%async_computation.30 | async-start | bytes 1671168 | tf_op jit(solution)/shard_map/reduce_scatter | solution.py:156
  393.9 563.5 %reduce-scatter.34.cloned.1.call-start = ((), (), s32[]{:S(2)}) async-start(), calls=%async_computation.29 | async-start | bytes 1671168 | tf_op jit(solution)/shard_map/reduce_scatter | solution.py:156
  405.7 579.2 %reduce-scatter.24.cloned.1.call-start = ((), (), s32[]{:S(2)}) async-start(), calls=%async_computation.24 | async-start | bytes 2359296 | tf_op jit(solution)/shard_map/reduce_scatter | solution.py:372
  414.9 705.9 %all-reduce.23.cloned.1.call-start = ((), (), s32[]{:S(2)}) async-start(), calls=%async_computation.31 | async-start | bytes 2097152 | tf_op jit(solution)/shard_map/psum | solution.py:414
  417.8 567.2 %copy-start.78 = (f32[1024]{0:T(1024)S(1)}, f32[1024]{0:T(1024)}, u32[]{:S(2)}) copy-start(f32[1024]{0:T(1024)} %param.28) | copy-start | bytes 12292
  417.8 567.2 %copy-start.102 = (f32[192]{0:T(256)S(1)}, f32[192]{0:T(256)}, u32[]{:S(2)}) copy-start(f32[192]{0:T(256)} %copy-done.101) | copy-start | bytes 2308
  420.6 565.8 %copy-start.106 = (f32[1024]{0:T(1024)S(1)}, f32[1024]{0:T(1024)}, u32[]{:S(2)}) copy-start(f32[1024]{0:T(1024)} %get-tuple-element.253) | copy-start | bytes 12292
  420.6 606.7 %copy-start.22 = (f32[192,1024]{1,0:T(8,128)S(1)}, f32[192,1024]{1,0:T(8,128)}, u32[]{:S(2)}) copy-start(f32[192,1024]{1,0:T(8,128)} %get-tuple-element.305) | copy-start | bytes 2359300
  420.6 606.7 %copy-start.125 = (f32[192]{0:T(256)S(1)}, f32[192]{0:T(256)}, u32[]{:S(2)}) copy-start(f32[192]{0:T(256)} %get-tuple-element.346) | copy-start | bytes 2308
  984.9 42.3 %copy-start.21 = (f32[192,1024]{1,0:T(8,128)S(1)}, f32[192,1024]{1,0:T(8,128)}, u32[]{:S(2)}) copy-start(f32[192,1024]{1,0:T(8,128)} %reduce-scatter.24.cloned.1.call-done) | copy-start | bytes 2359300
  (129 other events, 531.6 us)
Sparse Core Ops, SparseCore 0:
  9.6 22.5 all-gather.6
  33.7 20.3 all-gather.8
  55.7 21.2 all-gather.10
  122.1 32.7 reduce-scatter.17
  156.4 25.5 all-gather.12
  183.5 22.5 all-gather.14
  207.8 22.5 all-gather.16
  240.1 26.0 reduce-scatter.21
  268.5 17.4 reduce-scatter.19
  290.0 61.5 reduce-scatter.39
  355.3 60.5 reduce-scatter.41
  420.0 60.5 reduce-scatter.43
  484.1 54.2 reduce-scatter.45
  541.8 54.3 reduce-scatter.27
  599.5 54.3 reduce-scatter.29
  657.3 54.7 reduce-scatter.25
  715.9 54.7 reduce-scatter.31
  774.2 58.5 reduce-scatter.37
  836.9 58.5 reduce-scatter.35
  899.0 58.3 reduce-scatter.33
  959.8 25.1 reduce-scatter.23
  990.7 130.0 all-reduce.22

commit v2 on v1

--- a/solution.py
+++ b/solution.py
@@ -3,10 +3,14 @@
 import jax
 import jax.numpy as jnp
 from jax import lax
+from jax.experimental import pallas as pl
+from jax.experimental.pallas import tpu as pltpu
 from jax.sharding import PartitionSpec as P
 
 HEAD_DIMENSION = 64
 BLOCK = 128
+MESH = pl.DeviceIdType.MESH
+VMEM_LIMIT = 60 << 20
 
 
 top_precision = lax.Precision.HIGHEST
@@ -14,12 +18,8 @@
 rope_base = 100000000000.0
 
 
-def for_sending(shard):
-
-    def short(part):
-        return part.astype(jnp.bfloat16) if part.dtype == jnp.float32 else part
-
-    return jax.tree.map(short, shard)
+def low(values):
+    return values.astype(jnp.bfloat16)
 
 
 def dot_nt(first_mat, second_mat):
@@ -143,21 +143,392 @@
     return output_heads.reshape(length_total, head_count * head_size) * jax.nn.silu(gate_in)
 
 
-def gather_weights(weights):
-    return jax.tree.map(
-        lambda part, own: part.astype(own.dtype),
-        lax.all_gather(for_sending(weights), "fsdp", axis=0, tiled=True),
-        weights,
-    )
-
-
-def reduce_weight_grads(terms):
-    return [
-        lax.psum_scatter(
-            term.astype(jnp.bfloat16), ("grp", "fsdp"), scatter_dimension=0, tiled=True
-        ).astype(jnp.float32)
-        for term in terms
+def place():
+    g, f, t = lax.axis_index("grp"), lax.axis_index("fsdp"), lax.axis_index("tp")
+    return g, f // 2, f % 2, t
+
+
+def greet(devices):
+    barrier = pltpu.get_barrier_semaphore()
+    for device in devices:
+        pl.semaphore_signal(barrier, inc=1, device_id=device, device_id_type=MESH)
+    pl.semaphore_wait(barrier, len(devices))
+
+
+def remote(src, dst, send, recv, device):
+    return pltpu.make_async_remote_copy(
+        src_ref=src,
+        dst_ref=dst,
+        send_sem=send,
+        recv_sem=recv,
+        device_id=device,
+        device_id_type=MESH,
+    )
+
+
+def gather_body(units, groups, halves, *refs):
+    shards, own = refs[:units], refs[units : units + 2]
+    full, both = refs[units + 2 : 2 * units + 2], refs[2 * units + 2 : 2 * units + 4]
+    x_sems, z_sems, cx_sems, cz_sems, own_sems, local_sems, y_sems = refs[2 * units + 4 :]
+    g, hi, c, t = place()
+    f = hi * 2 + c
+    pair = g % 2
+    mate = g + 1 - 2 * pair
+    other_core, other_z, other_y = (g, hi * 2 + 1 - c, t), (mate, f, t), (g, f, 1 - t)
+    across = [(g, lax.rem(hi + k, halves) * 2 + c, t) for k in range(1, halves)]
+    greet([other_core, other_z, other_y] + across)
+    started = []
+
+    def start(copy):
+        copy.start()
+        started.append(copy)
+        return copy
+
+    def piece(ref, owner, part):
+        shard_rows = ref.shape[0] // (2 * halves)
+        half = shard_rows // 2
+        return ref.at[pl.ds(pl.multiple_of(owner * shard_rows + part * half, half), half), :]
+
+    def shard(ref, owner):
+        shard_rows = ref.shape[0] // (2 * halves)
+        return ref.at[pl.ds(pl.multiple_of(owner * shard_rows, shard_rows), shard_rows), :]
+
+    for i in range(2):
+        rows = own[i].shape[0]
+        where = pl.ds(pl.multiple_of(t * rows, rows), rows)
+        start(
+            remote(own[i], both[i].at[where, :], y_sems.at[0, i], y_sems.at[1, i], other_y)
+        )
+        local = pltpu.make_async_copy(own[i], both[i].at[where, :], local_sems.at[units + i])
+        local.start()
+        started.append(local)
+    arriving_x, arriving_z = {}, {}
+    for u in range(units):
+        half = shards[u].shape[0] // 2
+        mine = shards[u].at[pl.ds(pl.multiple_of(pair * half, half), half), :]
+        for k in range(1, halves):
+            arriving_x[u, k] = start(
+                remote(
+                    mine,
+                    piece(full[u], f, pair),
+                    x_sems.at[0, u, k],
+                    x_sems.at[1, u, k],
+                    across[k - 1],
+                )
+            )
+        start(
+            remote(
+                shards[u], shard(full[u], f), own_sems.at[0, u], own_sems.at[1, u], other_core
+            )
+        )
+        local = pltpu.make_async_copy(shards[u], shard(full[u], f), local_sems.at[u])
+        local.start()
+        started.append(local)
+    waiting = []
+    done_recv = set()
+    for u in range(units + 1):
+        if u < units:
+            for k in range(1, halves):
+                arriving_x[u, k].wait_recv()
+                done_recv.add(id(arriving_x[u, k]))
+                owner = lax.rem(hi - k + halves, halves) * 2 + c
+                block = piece(full[u], owner, pair)
+                arriving_z[u, k] = start(
+                    remote(block, block, z_sems.at[0, u, k], z_sems.at[1, u, k], other_z)
+                )
+                start(remote(block, block, cx_sems.at[0, u, k], cx_sems.at[1, u, k], other_core))
+        if u >= 1:
+            v = u - 1
+            for k in range(1, halves):
+                arriving_z[v, k].wait_recv()
+                done_recv.add(id(arriving_z[v, k]))
+                owner = lax.rem(hi - k + halves, halves) * 2 + c
+                block = piece(full[v], owner, 1 - pair)
+                start(remote(block, block, cz_sems.at[0, v, k], cz_sems.at[1, v, k], other_core))
+    for copy in started:
+        if id(copy) in done_recv:
+            copy.wait_send()
+        else:
+            copy.wait()
+
+
+def gather_all(weights, own_rows):
+    groups, halves = lax.axis_size("grp"), lax.axis_size("fsdp") // 2
+    units = len(weights)
+    anywhere = pl.BlockSpec(memory_space=pl.ANY)
+    shapes = [
+        jax.ShapeDtypeStruct((w.shape[0] * 2 * halves, w.shape[1]), w.dtype) for w in weights
+    ] + [jax.ShapeDtypeStruct((r.shape[0] * 2, r.shape[1]), r.dtype) for r in own_rows]
+    dma = pltpu.SemaphoreType.DMA
+    return pl.pallas_call(
+        partial(gather_body, units, groups, halves),
+        out_shape=shapes,
+        in_specs=[anywhere] * (units + 2),
+        out_specs=[anywhere] * (units + 2),
+        scratch_shapes=[
+            dma((2, units, halves)),
+            dma((2, units, halves)),
+            dma((2, units, halves)),
+            dma((2, units, halves)),
+            dma((2, units)),
+            dma((units + 2,)),
+            dma((2, 2)),
+        ],
+        compiler_params=pltpu.CompilerParams(
+            collective_id=0, has_side_effects=True, vmem_limit_bytes=VMEM_LIMIT
+        ),
+        name="gather_all",
+    )(*weights, *own_rows)
+
+
+def reduce_body(units, groups, halves, *refs):
+    parts, vector = refs[:units], refs[units]
+    sums, shared_sum, vector_sum = refs[units + 1 : 2 * units], refs[2 * units], refs[2 * units + 1]
+    base = 2 * units + 2
+    from_core, pair_sum = refs[base : base + units], refs[base + units : base + 2 * units]
+    base += 2 * units
+    from_x, chip_sum = refs[base : base + units], refs[base + units : base + 2 * units]
+    base += 2 * units
+    from_z = refs[base : base + units]
+    (
+        shared_y,
+        shared_all,
+        vec_core,
+        vec_x,
+        vec_y,
+        vec_z,
+        c_sems,
+        x_sems,
+        z_sems,
+        sy_sems,
+        sz_sems,
+        sx_sems,
+        sc_sems,
+        vc_sems,
+        vx_sems,
+        vy_sems,
+        vz_sems,
+    ) = refs[base + units :]
+    g, hi, c, t = place()
+    f = hi * 2 + c
+    other_core, other_y = (g, hi * 2 + 1 - c, t), (g, f, 1 - t)
+    across = [(g, lax.rem(hi + k, halves) * 2 + c, t) for k in range(1, halves)]
+    along = [(lax.rem(g + j, groups), f, t) for j in range(1, groups)]
+    greet([other_core, other_y] + across + along)
+    sending = []
+
+    def start(copy):
+        copy.start()
+        sending.append(copy)
+        return copy
+
+    core_copies = [
+        start(remote(parts[u].at[:, 1 - c], from_core[u], c_sems.at[0, u], c_sems.at[1, u], other_core))
+        for u in range(units)
     ]
+    vec_core[c] = vector[...]
+    vec_copy = start(remote(vector, vec_core.at[c], vc_sems.at[0], vc_sems.at[1], other_core))
+    x_copies, z_copies = {}, {}
+
+    def core_stage(u):
+        core_copies[u].wait_recv()
+
+        def add(i, carry):
+            gg, h = i // halves, lax.rem(i, halves)
+            pair_sum[u][h, gg] = (
+                parts[u][i, c].astype(jnp.float32) + from_core[u][i].astype(jnp.float32)
+            ).astype(jnp.bfloat16)
+            return carry
+
+        lax.fori_loop(0, groups * halves, add, 0)
+        for k in range(1, halves):
+            x_copies[u, k] = start(
+                remote(
+                    pair_sum[u].at[lax.rem(hi + k, halves)],
+                    from_x[u].at[k],
+                    x_sems.at[0, u, k],
+                    x_sems.at[1, u, k],
+                    across[k - 1],
+                )
+            )
+
+    def x_stage(u):
+        for k in range(1, halves):
+            x_copies[u, k].wait_recv()
+
+        def add(gg, carry):
+            total = pair_sum[u][hi, gg].astype(jnp.float32)
+            for k in range(1, halves):
+                total = total + from_x[u][k, gg].astype(jnp.float32)
+            chip_sum[u][gg] = total.astype(jnp.bfloat16)
+            return carry
+
+        lax.fori_loop(0, groups, add, 0)
+        for j in range(1, groups):
+            z_copies[u, j] = start(
+                remote(
+                    chip_sum[u].at[lax.rem(g + j, groups)],
+                    from_z[u].at[j],
+                    z_sems.at[0, u, j],
+                    z_sems.at[1, u, j],
+                    along[j - 1],
+                )
+            )
+
+    def z_stage(u):
+        for j in range(1, groups):
+            z_copies[u, j].wait_recv()
+        total = chip_sum[u][g].astype(jnp.float32)
+        for j in range(1, groups):
+            total = total + from_z[u][j].astype(jnp.float32)
+        return total
+
+    core_stage(0)
+    vec_copy.wait_recv()
+    vec_x[hi] = vec_core[0] + vec_core[1]
+    vec_copies = [
+        start(remote(vec_x.at[hi], vec_x.at[hi], vx_sems.at[0, k], vx_sems.at[1, k], across[k - 1]))
+        for k in range(1, halves)
+    ]
+    core_stage(1)
+    for copy in vec_copies:
+        copy.wait_recv()
+    total = vec_x[0]
+    for h in range(1, halves):
+        total = total + vec_x[h]
+    vec_y[t] = total
+    vec_copy = start(remote(vec_y.at[t], vec_y.at[t], vy_sems.at[0], vy_sems.at[1], other_y))
+    x_stage(0)
+    core_stage(2)
+    vec_copy.wait_recv()
+    vec_z[g] = vec_y[0] + vec_y[1]
+    vec_copies = [
+        start(remote(vec_z.at[g], vec_z.at[g], vz_sems.at[0, j], vz_sems.at[1, j], along[j - 1]))
+        for j in range(1, groups)
+    ]
+    for u in range(3, units + 2):
+        if u < units:
+            core_stage(u)
+        if u - 2 < units and u >= 3:
+            x_stage(u - 2)
+        if u == 4:
+            shared_y[t] = z_stage(0)
+            shared_copy = start(
+                remote(shared_y.at[t], shared_y.at[t], sy_sems.at[0], sy_sems.at[1], other_y)
+            )
+        if u == 5:
+            for copy in vec_copies:
+                copy.wait_recv()
+            total = vec_z[0]
+            for j in range(1, groups):
+                total = total + vec_z[j]
+            vector_sum[...] = total
+            shared_copy.wait_recv()
+            shared_all[g, hi, c] = (shared_y[0] + shared_y[1]).astype(jnp.bfloat16)
+            sz = [
+                start(
+                    remote(
+                        shared_all.at[g, hi, c],
+                        shared_all.at[g, hi, c],
+                        sz_sems.at[0, j],
+                        sz_sems.at[1, j],
+                        along[j - 1],
+                    )
+                )
+                for j in range(1, groups)
+            ]
+        if u == 6:
+            for copy in sz:
+                copy.wait_recv()
+            sx = [
+                start(
+                    remote(
+                        shared_all.at[:, hi, c],
+                        shared_all.at[:, hi, c],
+                        sx_sems.at[0, k],
+                        sx_sems.at[1, k],
+                        across[k - 1],
+                    )
+                )
+                for k in range(1, halves)
+            ]
+        if u == 7:
+            for copy in sx:
+                copy.wait_recv()
+            sc = start(
+                remote(
+                    shared_all.at[:, :, c],
+                    shared_all.at[:, :, c],
+                    sc_sems.at[0],
+                    sc_sems.at[1],
+                    other_core,
+                )
+            )
+        if u >= 5:
+            sums[u - 5][...] = z_stage(u - 4)
+    for v in range(units - 2, units):
+        sums[v - 1][...] = z_stage(v)
+    sc.wait_recv()
+
+    def widen(i, carry):
+        shared_sum[i] = shared_all[
+            i // (2 * halves), lax.rem(i // 2, halves), lax.rem(i, 2)
+        ].astype(jnp.float32)
+        return carry
+
+    lax.fori_loop(0, groups * halves * 2, widen, 0)
+    for copy in sending:
+        copy.wait_send()
+
+
+def reduce_all(parts, vector):
+    groups, halves = lax.axis_size("grp"), lax.axis_size("fsdp") // 2
+    units = len(parts)
+    blocks = groups * halves * 2
+    rows = parts[0].shape[0] // blocks
+    widths = [p.shape[1] for p in parts]
+    f32, bf16 = jnp.float32, jnp.bfloat16
+    inside = pl.BlockSpec(memory_space=pltpu.VMEM)
+    dma = pltpu.SemaphoreType.DMA
+    outs = pl.pallas_call(
+        partial(reduce_body, units, groups, halves),
+        out_shape=[jax.ShapeDtypeStruct((rows, w), f32) for w in widths[1:]]
+        + [
+            jax.ShapeDtypeStruct((blocks, rows, widths[0]), f32),
+            jax.ShapeDtypeStruct(vector.shape, f32),
+        ],
+        in_specs=[inside] * (units + 1),
+        out_specs=[inside] * (units + 1),
+        scratch_shapes=[pltpu.VMEM((groups * halves, rows, w), bf16) for w in widths]
+        + [pltpu.VMEM((halves, groups, rows, w), bf16) for w in widths]
+        + [pltpu.VMEM((halves, groups, rows, w), bf16) for w in widths]
+        + [pltpu.VMEM((groups, rows, w), bf16) for w in widths]
+        + [pltpu.VMEM((groups, rows, w), bf16) for w in widths]
+        + [
+            pltpu.VMEM((2, rows, widths[0]), f32),
+            pltpu.VMEM((groups, halves, 2, rows, widths[0]), bf16),
+            pltpu.VMEM((2,) + vector.shape, f32),
+            pltpu.VMEM((halves,) + vector.shape, f32),
+            pltpu.VMEM((2,) + vector.shape, f32),
+            pltpu.VMEM((groups,) + vector.shape, f32),
+            dma((2, units)),
+            dma((2, units, halves)),
+            dma((2, units, groups)),
+            dma((2,)),
+            dma((2, groups)),
+            dma((2, halves)),
+            dma((2,)),
+            dma((2,)),
+            dma((2, halves)),
+            dma((2,)),
+            dma((2, groups)),
+        ],
+        compiler_params=pltpu.CompilerParams(
+            collective_id=1, has_side_effects=True, vmem_limit_bytes=VMEM_LIMIT
+        ),
+        name="reduce_all",
+    )(*[p.reshape(blocks // 2, 2, rows, p.shape[1]) for p in parts], vector)
+    return outs[: units - 1], outs[units - 1].reshape(blocks * rows, widths[0]), outs[units]
 
 
 def local(
@@ -198,15 +569,26 @@
     first_normalized = (resid_in * scale_one * norm1_gain).astype(jnp.bfloat16)
     top_grad = out_grad.astype(jnp.float32) * valid_own
     top_grad_low = top_grad.astype(jnp.bfloat16)
-    normed1_all, top_grad_all = (
-        lax.all_gather(first_normalized, "tp", axis=0, tiled=True),
-        lax.all_gather(top_grad_low, "tp", axis=0, tiled=True),
-    )
-    mixer_full = gather_weights(
-        (w_query, key_weight, value_weight, w_attn_out, w_mamba_z, w_mamba_x, w_step, w_mamba_out)
-    )
-    ffn_full = gather_weights((w_ffn_gate, w_ffn_up, w_ffn_down))
-    wq_all, wk_all, wv_all, wo_all, wz_all, wx_all, wdt_all, wout_all = mixer_full
+    q_width, kv_width, step_width = w_query.shape[1], key_weight.shape[1], w_step.shape[1]
+    narrow = jnp.concatenate(
+        [
+            w_query,
+            key_weight,
+            value_weight,
+            jnp.pad(w_step, ((0, 0), (0, 128 - step_width))),
+        ],
+        axis=1,
+    )
+    narrow_all, wx_all, wz_all, wo_all, wout_all, wg_all, wu_all, wd_all, normed1_all, top_grad_all = (
+        gather_all(
+            (narrow, w_mamba_x, w_mamba_z, w_attn_out, w_mamba_out, w_ffn_gate, w_ffn_up, w_ffn_down),
+            (first_normalized, top_grad_low),
+        )
+    )
+    wq_all = narrow_all[:, :q_width]
+    wk_all = narrow_all[:, q_width : q_width + kv_width]
+    wv_all = narrow_all[:, q_width + kv_width : q_width + 2 * kv_width]
+    wdt_all = narrow_all[:, q_width + 2 * kv_width : q_width + 2 * kv_width + step_width]
     q_local = wq_all.shape[1] // HEAD_DIMENSION
     kv_local = wk_all.shape[1] // HEAD_DIMENSION
     grouping = q_local // kv_local
@@ -266,7 +648,6 @@
     scale_two = rms_scale(resid_mid)
     normed2 = (resid_mid * scale_two * norm2_gain).astype(jnp.bfloat16)
     normed2_all = lax.all_gather(normed2, "tp", axis=0, tiled=True)
-    wg_all, wu_all, wd_all = ffn_full
     gate_pre = jnp.dot(normed2_all, wg_all, preferred_element_type=jnp.float32)
     up_pre = jnp.dot(normed2_all, wu_all, preferred_element_type=jnp.float32)
     sigma_gate = jax.nn.sigmoid(gate_pre)
@@ -277,20 +658,17 @@
         ffn_part.astype(jnp.bfloat16), "tp", scatter_dimension=0, tiled=True
     ).astype(jnp.float32)
     output = ((resid_mid + ffn_sum) * valid_own).astype(jnp.bfloat16)
-    ffn_back = ffn_full
-    wg_back, wu_back, wd_back = ffn_back
+    wg_back, wu_back, wd_back = wg_all, wu_all, wd_all
     hidden_grad = jnp.dot(top_grad_all, wd_back, preferred_element_type=jnp.float32)
     silu_slope = sigma_gate * (1.0 + gate_pre * (1.0 - sigma_gate))
     gate_grad = (hidden_grad * up_pre * silu_slope).astype(jnp.bfloat16)
     up_grad = (hidden_grad * silu_gate).astype(jnp.bfloat16)
 
-    ffn_grads = reduce_weight_grads(
-        [
-            dot_tn(normed2_all, gate_grad),
-            dot_tn(normed2_all, up_grad),
-            dot_tn(top_grad_all, hidden_low),
-        ]
-    )
+    ffn_grads = [
+        low(dot_tn(normed2_all, gate_grad)),
+        low(dot_tn(normed2_all, up_grad)),
+        low(dot_tn(top_grad_all, hidden_low)),
+    ]
     norm2_part = dot_nt(gate_grad, wg_back) + dot_nt(up_grad, wu_back)
     norm2_grad = lax.psum_scatter(norm2_part, "tp", scatter_dimension=0, tiled=True)
     gain2_part = jnp.sum(norm2_grad * resid_mid * scale_two, axis=0)
@@ -302,8 +680,8 @@
     )
     mix_grad_low = resid_grad.astype(jnp.bfloat16)
     mix_grad_all = lax.all_gather(mix_grad_low, "tp", axis=0, tiled=True)
-    mixer_back = mixer_full
-    wq_back, wk_back, wv_back, wo_back, wz_back, wx_back, wdt_back, wout_back = mixer_back
+    wq_back, wk_back, wv_back, wo_back = wq_all, wk_all, wv_all, wo_all
+    wz_back, wx_back, wdt_back, wout_back = wz_all, wx_all, wdt_all, wout_all
     attn_grad = jnp.dot(mix_grad_all, wo_back, preferred_element_type=jnp.float32).astype(
         jnp.bfloat16
     )
@@ -379,18 +757,22 @@
     )
     grad_in = input_grad.astype(jnp.bfloat16)
 
-    mixer_parts = reduce_weight_grads(
+    narrow_back = jnp.concatenate(
         [
-            dot_tn(normed1_all, query_back),
-            dot_tn(normed1_all, key_back),
-            dot_tn(normed1_all, value_back),
-            dot_tn(mix_grad_all, attn_low),
-            dot_tn(normed1_all, gate_back_low),
-            dot_tn(normed1_all, main_back_low),
-            dot_tn(normed1_all, step_back_low),
-            dot_tn(mix_grad_all, mamba_low),
-        ]
-    )
+            query_back,
+            key_back,
+            value_back,
+            jnp.pad(step_back_low, ((0, 0), (0, 128 - step_width))),
+        ],
+        axis=1,
+    )
+    mixer_grads = [
+        low(dot_tn(mix_grad_all, attn_low)),
+        low(dot_tn(mix_grad_all, mamba_low)),
+        low(dot_tn(normed1_all, gate_back_low)),
+        low(dot_tn(normed1_all, main_back_low)),
+        low(dot_tn(normed1_all, narrow_back)),
+    ]
     shared_w_grad = lax.dot_general(
         normed1_all.astype(jnp.float32),
         shared_back,
@@ -410,43 +792,49 @@
     skip_full = lax.dynamic_update_slice_in_dim(
         jnp.zeros(skip_gain.shape, jnp.float32), skip_grad, tp_rank * heads_local, 0
     )
-    gain1_sum, shared_sum, kernel_sum, conv_shared_sum, decay_sum, bias_sum, skip_sum, gain2_sum = (
-        lax.psum(
-            (
-                gain1_part,
-                shared_w_grad,
-                kernel_full,
-                conv_shared_grad,
-                decay_full,
-                bias_full,
-                skip_full,
-                gain2_part,
-            ),
-            ("grp", "fsdp", "tp"),
-        )
-    )
+    pieces = [
+        gain1_part,
+        gain2_part,
+        conv_shared_grad,
+        kernel_full,
+        decay_full,
+        bias_full,
+        skip_full,
+    ]
+    flat = jnp.concatenate([p.reshape(-1) for p in pieces])
+    vector = jnp.pad(flat, (0, -flat.shape[0] % 1024)).reshape(-1, 128)
+    wide_sums, shared_sum, vector_sum = reduce_all(
+        [low(shared_w_grad)] + ffn_grads + mixer_grads, vector
+    )
+    vector_sum = vector_sum.reshape(-1)
+    small, at = [], 0
+    for p in pieces:
+        small.append(vector_sum[at : at + p.size].reshape(p.shape))
+        at += p.size
+    gain1_sum, gain2_sum, conv_shared_sum, kernel_sum, decay_sum, bias_sum, skip_sum = small
+    gate_sum, up_sum, down_sum, attn_out_sum, mamba_out_sum, z_sum, x_sum, narrow_sum = wide_sums
     return (
         output,
         grad_in,
         gain1_sum,
-        mixer_parts[0],
-        mixer_parts[1],
-        mixer_parts[2],
-        mixer_parts[3],
-        mixer_parts[4],
-        mixer_parts[5],
-        mixer_parts[6],
+        narrow_sum[:, :q_width],
+        narrow_sum[:, q_width : q_width + kv_width],
+        narrow_sum[:, q_width + kv_width : q_width + 2 * kv_width],
+        attn_out_sum,
+        z_sum,
+        x_sum,
+        narrow_sum[:, q_width + 2 * kv_width : q_width + 2 * kv_width + step_width],
         shared_sum,
         kernel_sum,
         conv_shared_sum,
         decay_sum,
         bias_sum,
         skip_sum,
-        mixer_parts[7],
+        mamba_out_sum,
         gain2_sum,
-        ffn_grads[0],
-        ffn_grads[1],
-        ffn_grads[2],
+        gate_sum,
+        up_sum,
+        down_sum,
     )
 
 

time: 1140 us -> 566 us (0.50)
  waiting for transfers between devices: 740 us -> 69.7 us
  Pallas kernels: 0 us -> 233 us
  blocking collectives: 128 us -> 23.2 us
  matrix products: 126 us -> 103 us
  other arithmetic: 63.4 us -> 47.8 us
  local copies, waits for them, and re-layouts: 54.4 us -> 66.8 us
    reduce_scatter x10 -> x0, waiting for transfers between devices: 467 us -> none  [reduce_weight_grads(): lax.psum_scatter(term.astype(jnp.bfloat16), ('grp', 'fsdp'), scatter_dime...]
    pallas_call x0 -> x2, Pallas kernels: none -> 233 us  [the longest x1 125 us: gather_all(): pl.pallas_call(partial(gather_body, units, groups, halves), out_shape=sha...]
    psum x1 -> x0, waiting for transfers between devices: 92.5 us -> none  [local(): lax.psum((gain1_part, shared_w_grad, kernel_full, conv_shared_grad, decay...]
    all_gather x7 -> x0, blocking collectives: 63 us -> none  [the longest x5 34 us: gather_weights(): lax.all_gather(for_sending(weights), 'fsdp', axis=0, tiled=True)]
    unnamed x23 -> x4, waiting for transfers between devices: 60.3 us -> 0.07 us
    all_gather x6 -> x0, waiting for transfers between devices: 52.8 us -> none  [gather_weights(): lax.all_gather(for_sending(weights), 'fsdp', axis=0, tiled=True)]
    psum x1 -> x0, blocking collectives: 40.9 us -> none  [local(): lax.psum((gain1_part, shared_w_grad, kernel_full, conv_shared_grad, decay...]
    reduce_scatter x1, waiting for transfers between devices: 25.9 us -> 3.9 us  [local(): lax.psum_scatter(norm1_part, 'tp', scatter_dimension=0, tiled=True)]
  transfers between devices with their start and end apart: 22 -> 4, of which waited for: 17 -> 4; matrix products, arithmetic and copies ran while one was open for 19% -> 5% of each run, Pallas kernels for 0% -> 0%
where the time goes in v2:
time: 566 us; the launch traced here: 561 us
  Pallas kernels  233 us (41%)
  matrix products  103 us (18%)
  waiting for transfers between devices  69.7 us (12%)
  local copies, waits for them, and re-layouts  66.8 us (12%)
  other arithmetic  47.8 us (8%)
  blocking collectives  23.2 us (4%)
  between operations  16.4 us (3%)
    pallas_call x1, Pallas kernels, gather_all(): pl.pallas_call(partial(gather_body, units, groups, halves), out_shape=sha...  125 us
    pallas_call x1, Pallas kernels, reduce_all(): pl.pallas_call(partial(reduce_body, units, groups, halves), out_shape=[ja...  109 us
    reduce_scatter x1, waiting for transfers between devices, local(): mixed = lax.psum_scatter(mix_part, 'tp', scatter_dimension=0, tiled=True)  26.4 us
    reduce_scatter x1, waiting for transfers between devices, local(): lax.psum_scatter(norm2_part, 'tp', scatter_dimension=0, tiled=True)  22.4 us
    dot_general x11, matrix products, dot_nt(): lax.dot_general(first_mat, second_mat, (((1,), (1,)), ((), ())), preferre...  19.6 us
    dot_general x8, matrix products, dot_tn(): lax.dot_general(first_mat, second_mat, (((0,), (0,)), ((), ())), preferre...  18.9 us
    unnamed x361, local copies, waits for them, and re-layouts  17.2 us
    reduce_scatter x1, waiting for transfers between devices, local(): lax.psum_scatter(ffn_part.astype(jnp.bfloat16), 'tp', scatter_dimension=0...  16.9 us
  transfers between devices with their start and end apart: 4, of which 4 were waited for; matrix products, arithmetic and copies ran while one was open for 5% of the time, Pallas kernels for 0%

profile of v2, /device:TPU:0, one launch (start us, length us, event | category | flops | bytes accessed | tf_op | source)
XLA Modules:
  0.0 560.5 jit_solution(15948125991039115225)
XLA Ops:
  17.3 124.7 %gather_all.1 = (bf16[1024,512]{1,0:T(8,128)(2,1)}, bf16[1024,768]{1,0:T(8,128)(2,1)}, bf16[1024,768]{1,0:T(8,128)(2,1)}, bf16[1024,256]{1,0:T(8,128)(2,1)}, bf1...) custom-call(bf16[256,512]{1,0:T(8,128)(2,1)} %fusion.124.refs_0_, ...), custom_call_target="tpu_custom_call" | custom-call | tf_op jit(solution)/shard_map/gather_all/pallas_call | solution.py:263
  155.2 2.7 copy.132
  164.1 9.3 %while.34 = (s32[]{:T(128)}, f32[12,64,128]{2,1,0:T(8,128)S(1)}, f32[3,12,64,128]{3,2,1,0:T(8,128)S(1)}, f32[3,12,1,1]{1,3,2,0:T(1,128)}, f32[3,12]{1,0:T(4,128)...) while((s32[]{:T(128)}, f32[12,64,128]{2,1,0:T(8,128)S(1)}, ...), condition=%wide.region_4.5_spmd.clone, body=%wide.region_3.4_spmd.clone.sunk | while | flops 393219 | bytes 1967868 | solution.py:109
  175.7 5.9 %fusion.27 = f32[3,128,12,64]{1,3,2,0:T(8,128)} fusion(f32[3,128,12,64]{1,3,2,0:T(8,128)S(1)} %fusion.206, f32[3,128,12]{1,2,0:T(8,128)S(1)} %copy-done.120, f32[3,128,128]{2,1,0:T(8,128)S(1)} %fusion.205, f32[3,128,12]{1,2,0:T(8,128)S(1)} %convolution_bitcast_fusion.5, pred[128,128]{1,0:T(8,128)(4,1)S(1)} %copy-done.135, f32[3,128,12]{1,2,0:T(8,128)S(1)} %copy-done.79, ...), kind=kOutput, calls=%fused_computation.60 | convolution fusion | flops 456523776 | bytes 3807232 | tf_op jit(solution)/shard_map/jvp(ctsh,cshp->cthp)/dot_general | solution.py:100
  181.5 3.3 copy.172
  184.8 3.7 reshape.537
  199.2 26.4 %reduce-scatter.5.cloned.1.call-done = f32[192,1024]{1,0:T(8,128)} async-done(((f32[384,1024]{1,0:T(8,128)}), f32[192,1024]{1,0:T(8,128)}) %reduce-scatter.5.cloned.1.call-update) | async-done | bytes 786448 | tf_op jit(solution)/shard_map/reduce_scatter | solution.py:646
  229.6 11.5 %all_gather.6 = bf16[384,1024]{1,0:T(8,128)(2,1)S(1)} all-gather(bf16[192,1024]{1,0:T(8,128)(2,1)S(1)} %multiply_convert_fusion.5), channel_id=1, replica_groups=mesh['grp'=4,'fsdp'=4,'tp'=2] {'tp'}, dimensions={0}, use_global_device_ids=true | all-gather | bytes 1179648 | tf_op jit(solution)/shard_map/all_gather | solution.py:650
  250.6 3.7 convolution_convert_fusion.7
  254.5 22.4 %reduce-scatter.9.cloned.1.call-done = f32[192,1024]{1,0:T(8,128)} async-done(((f32[384,1024]{1,0:T(8,128)}), f32[192,1024]{1,0:T(8,128)}) %reduce-scatter.9.cloned.1.call-update) | async-done | bytes 786448 | tf_op jit(solution)/shard_map/reduce_scatter | solution.py:673
  279.6 16.9 %reduce-scatter.7.cloned.1.call-done = bf16[192,1024]{1,0:T(8,128)(2,1)} async-done(((bf16[384,1024]{1,0:T(8,128)(2,1)}), bf16[192,1024]{1,0:T(8,128)(2,1)}) %reduce-scatter.7.cloned.1.call-update) | async-done | bytes 393232 | tf_op jit(solution)/shard_map/reduce_scatter | solution.py:657
  296.6 3.1 fusion.196
  299.7 11.7 %all_gather.7 = bf16[384,1024]{1,0:T(8,128)(2,1)S(1)} all-gather(bf16[192,1024]{1,0:T(8,128)(2,1)S(1)} %get-tuple-element.421), channel_id=1, replica_groups=mesh['grp'=4,'fsdp'=4,'tp'=2] {'tp'}, dimensions={0}, use_global_device_ids=true | all-gather | bytes 1179648 | tf_op jit(solution)/shard_map/all_gather | solution.py:682
  311.4 3.2 multiply_reduce_fusion.2
  314.7 2.7 copy.143
  317.3 2.8 reshape.495
  320.1 3.7 fusion.75
  323.8 2.7 convolution_bitcast_fusion.1
  328.3 11.8 %while.35 = (s32[]{:T(128)}, f32[12,64,128]{2,1,0:T(8,128)S(1)}, f32[3,12]{1,0:T(4,128)}, f32[3,12,64,128]{3,2,1,0:T(8,128)}, f32[3,12,64,128]{3,2,1,0:T(8,128)}...) while((s32[]{:T(128)}, f32[12,64,128]{2,1,0:T(8,128)S(1)}, ...), condition=%wide.region_13.14_spmd.clone, body=%wide.region_11.13_spmd.clone.sunk | while | flops 589816 | bytes 2359724 | solution.py:109
  340.1 2.6 fusion.211
  342.9 3.5 convolution_bitcast_fusion
  353.7 6.6 %fusion.31 = (f32[3,128,12]{1,2,0:T(8,128)}, f32[3,128,12]{1,2,0:T(8,128)}, f32[3,128,12]{1,2,0:T(8,128)}, f32[3,128,128]{2,1,0:T(8,128)S(1)}) fusion(f32[3,128,12]{1,2,0:T(8,128)S(1)} %copy-done.121, f32[3,128,128]{2,1,0:T(8,128)S(1)} %copy-done.89, f32[3,128,12]{1,2,0:T(8,128)S(1)} %copy-done.72, pred[128,128]{1,0:T(8,128)(4,1)S(1)} %copy-done.136, ...), kind=kOutput, calls=%fused_computation.64 | convolution fusion | flops 461769216 | bytes 2861056 | tf_op jit(solution)/shard_map/transpose(jvp(ctsh,cshp->cthp))/dot_general | solution.py:100
  360.3 3.8 fusion.24
  365.6 3.3 copy.173
  368.9 3.5 reshape.538
  372.4 5.4 multiply_reduce_fusion.6
  397.0 4.0 add_add_fusion
  401.0 4.1 convolution_convert_fusion.2
  405.1 2.6 convolution_convert_fusion.1
  407.9 2.6 convolution_convert_fusion
  423.3 3.9 reduce-scatter.11.cloned.1.call-done
  429.3 108.6 %reduce_all.1 = (f32[64,1024]{1,0:T(8,128)}, f32[64,1024]{1,0:T(8,128)}, f32[64,1024]{1,0:T(8,128)}, f32[64,256]{1,0:T(8,128)}, f32[64,768]{1,0:T(8,128)}, /*ind...) custom-call(bf16[8,2,64,256]{3,2,1,0:T(8,128)(2,1)} %bitcast.327, ...), custom_call_target="tpu_custom_call" | custom-call | tf_op jit(solution)/shard_map/reduce_all/pallas_call | solution.py:493
  (521 shorter events, 138.3 us)
Async XLA Ops:
  7.2 153.0 %copy-start = (bf16[1024,256]{1,0:T(8,128)(2,1)S(1)}, bf16[1024,256]{1,0:T(8,128)(2,1)}, u32[]{:S(2)}) copy-start(bf16[1024,256]{1,0:T(8,128)(2,1)} %param.36) | copy-start | bytes 1572868
  7.2 7.6 %copy-start.7 = (bf16[192,1024]{1,0:T(8,128)(2,1)S(1)}, bf16[192,1024]{1,0:T(8,128)(2,1)}, u32[]{:S(2)}) copy-start(bf16[192,1024]{1,0:T(8,128)(2,1)} %param.26) | copy-start | bytes 1179652
  7.2 9.2 %copy-start.168 = (f32[24]{0:T(128)S(1)}, f32[24]{0:T(128)}, u32[]{:S(2)}) copy-start(f32[24]{0:T(128)} %param.40) | copy-start | bytes 292
  7.2 9.3 %copy-start.90 = (bf16[256,256]{1,0:T(8,128)(2,1)S(1)}, bf16[256,256]{1,0:T(8,128)(2,1)}, u32[]{:S(2)}) copy-start(bf16[256,256]{1,0:T(8,128)(2,1)} %param.29) | copy-start | bytes 393220
  7.2 218.4 %reduce-scatter.5.cloned.1.call-start = ((), (), s32[]{:S(2)}) async-start(), calls=%async_computation.4 | async-start | bytes 2359296 | tf_op jit(solution)/shard_map/reduce_scatter | solution.py:646
  8.5 133.6 %copy-start.114 = (f32[384]{0:T(512)}, f32[384]{0:T(512)S(1)}, u32[]{:S(2)}) copy-start(f32[384]{0:T(512)S(1)} %get-tuple-element.484) | copy-start | bytes 4612
  10.3 7.0 %copy-start.125 = (f32[192]{0:T(256)}, f32[192]{0:T(256)S(1)}, u32[]{:S(2)}) copy-start(f32[192]{0:T(256)S(1)} %get-tuple-element.472) | copy-start | bytes 2308
  17.3 127.0 %copy-start.162 = (f32[24]{0:T(128)S(1)}, f32[24]{0:T(128)}, u32[]{:S(2)}) copy-start(f32[24]{0:T(128)} %param.39) | copy-start | bytes 292
  142.1 7.9 %copy-start.13 = (bf16[1024,512]{1,0:T(8,128)(2,1)S(1)}, bf16[1024,512]{1,0:T(8,128)(2,1)}, u32[]{:S(2)}) copy-start(bf16[1024,512]{1,0:T(8,128)(2,1)} %get-tuple-element.217) | copy-start | bytes 3145732
  145.0 30.1 %copy-start.71 = (f32[3,128,12]{1,2,0:T(8,128)}, f32[3,128,12]{1,2,0:T(8,128)S(1)}, u32[]{:S(2)}) copy-start(f32[3,128,12]{1,2,0:T(8,128)S(1)} %convolution_bitcast_fusion.5) | copy-start | bytes 55300
  145.8 15.9 %copy-start.77 = (f32[3,128,12]{1,2,0:T(8,128)}, f32[3,128,12]{1,2,0:T(8,128)S(1)}, u32[]{:S(2)}) copy-start(f32[3,128,12]{1,2,0:T(8,128)S(1)} %get-tuple-element.463) | copy-start | bytes 55300
  149.5 40.2 %copy-start.112 = (f32[384]{0:T(512)}, f32[384]{0:T(512)S(1)}, u32[]{:S(2)}) copy-start(f32[384]{0:T(512)S(1)} %iota_convert_fusion) | copy-start | bytes 4612
  175.1 6.4 %copy-start.88 = (f32[3,128,128]{2,1,0:T(8,128)}, f32[3,128,128]{2,1,0:T(8,128)S(1)}, u32[]{:S(2)}) copy-start(f32[3,128,128]{2,1,0:T(8,128)S(1)} %fusion.205) | copy-start | bytes 589828
  199.1 26.5 %copy-start.8 = (bf16[192,1024]{1,0:T(8,128)(2,1)S(1)}, bf16[192,1024]{1,0:T(8,128)(2,1)}, u32[]{:S(2)}) copy-start(bf16[192,1024]{1,0:T(8,128)(2,1)} %param.26) | copy-start | bytes 1179652
  199.1 29.2 %copy-start.105 = (f32[1024]{0:T(1024)S(1)}, f32[1024]{0:T(1024)}, u32[]{:S(2)}) copy-start(f32[1024]{0:T(1024)} %param.43) | copy-start | bytes 12292
  199.1 77.7 %reduce-scatter.9.cloned.1.call-start = ((), (), s32[]{:S(2)}) async-start(), calls=%async_computation.6 | async-start | bytes 2359296 | tf_op jit(solution)/shard_map/reduce_scatter | solution.py:673
  227.7 13.5 %copy-start.32 = (bf16[1024,1024]{1,0:T(8,128)(2,1)S(1)}, bf16[1024,1024]{1,0:T(8,128)(2,1)}, u32[]{:S(2)}) copy-start(bf16[1024,1024]{1,0:T(8,128)(2,1)} %get-tuple-element.224) | copy-start | bytes 6291460
  228.3 12.9 %copy-start.137 = (f32[192]{0:T(256)}, f32[192]{0:T(256)S(1)}, u32[]{:S(2)}) copy-start(f32[192]{0:T(256)S(1)} %get-tuple-element.474) | copy-start | bytes 2308
  250.6 45.9 %reduce-scatter.7.cloned.1.call-start = ((), (), s32[]{:S(2)}) async-start(), calls=%async_computation.5 | async-start | bytes 1179648 | tf_op jit(solution)/shard_map/reduce_scatter | solution.py:657
  254.4 172.8 %reduce-scatter.11.cloned.1.call-start = ((), (), s32[]{:S(2)}) async-start(), calls=%async_computation.7 | async-start | bytes 2359296 | tf_op jit(solution)/shard_map/reduce_scatter | solution.py:750
  296.5 14.8 %copy-start.23 = (f32[384,768]{1,0:T(8,128)S(1)}, f32[384,768]{1,0:T(8,128)}, u32[]{:S(2)}) copy-start(f32[384,768]{1,0:T(8,128)} %get-tuple-element.426) | copy-start | bytes 3538948
  296.5 14.8 %copy-start.46 = (bf16[1024,768]{1,0:T(8,128)(2,1)S(1)}, bf16[1024,768]{1,0:T(8,128)(2,1)}, u32[]{:S(2)}) copy-start(bf16[1024,768]{1,0:T(8,128)(2,1)} %get-tuple-element.222) | copy-start | bytes 4718596
  296.5 14.8 %copy-start.50 = (f32[384,768]{1,0:T(8,128)S(1)}, f32[384,768]{1,0:T(8,128)}, u32[]{:S(2)}) copy-start(f32[384,768]{1,0:T(8,128)} %reshape.537) | copy-start | bytes 3538948
  296.5 14.9 %copy-start.129 = (f32[768]{0:T(1024)S(1)}, f32[768]{0:T(1024)}, u32[]{:S(2)}) copy-start(f32[768]{0:T(1024)} %mul.921) | copy-start | bytes 9220
  296.5 14.9 %copy-start.172 = (f32[384,768]{1,0:T(8,128)S(1)}, f32[384,768]{1,0:T(8,128)}, u32[]{:S(2)}) copy-start(f32[384,768]{1,0:T(8,128)} %get-tuple-element.480) | copy-start | bytes 3538948
  421.1 7.5 %copy-start.127 = (f32[1024]{0:T(1024)S(1)}, f32[1024]{0:T(1024)}, u32[]{:S(2)}) copy-start(f32[1024]{0:T(1024)} %get-tuple-element.377) | copy-start | bytes 12292
  429.3 117.7 %copy-start.28 = (f32[192,1024]{1,0:T(8,128)S(1)}, f32[192,1024]{1,0:T(8,128)}, u32[]{:S(2)}) copy-start(f32[192,1024]{1,0:T(8,128)} %reduce-scatter.11.cloned.1.call-done) | copy-start | bytes 2359300
  429.3 117.7 %copy-start.29 = (f32[192,1024]{1,0:T(8,128)S(1)}, f32[192,1024]{1,0:T(8,128)}, u32[]{:S(2)}) copy-start(f32[192,1024]{1,0:T(8,128)} %get-tuple-element.422) | copy-start | bytes 2359300
  429.3 117.7 %copy-start.151 = (f32[192]{0:T(256)S(1)}, f32[192]{0:T(256)}, u32[]{:S(2)}) copy-start(f32[192]{0:T(256)} %get-tuple-element.471) | copy-start | bytes 2308
  537.9 10.2 %copy-start.97 = (f32[64,256]{1,0:T(8,128)S(1)}, f32[64,256]{1,0:T(8,128)}, u32[]{:S(2)}) copy-start(f32[64,256]{1,0:T(8,128)} %get-tuple-element.652) | copy-start | bytes 196612
  537.9 10.8 %copy-start.87 = (f32[64,768]{1,0:T(8,128)S(1)}, f32[64,768]{1,0:T(8,128)}, u32[]{:S(2)}) copy-start(f32[64,768]{1,0:T(8,128)} %get-tuple-element.653) | copy-start | bytes 589828
  540.9 8.5 %copy-start.86 = (f32[64,768]{1,0:T(8,128)S(1)}, f32[64,768]{1,0:T(8,128)}, u32[]{:S(2)}) copy-start(f32[64,768]{1,0:T(8,128)} %get-tuple-element.654) | copy-start | bytes 589828
  (145 other events, 367.5 us)
Sparse Core Ops, SparseCore 0:
  199.2 26.2 reduce-scatter.4
  250.7 26.0 reduce-scatter.8
  279.1 17.4 reduce-scatter.6
  401.1 26.0 reduce-scatter.10
